TPU v7x, 32 devices: a whole 2x2x4 slice. The times are simulated.
32 devices in a mesh: blk: 4 (over y, core), seq: 8 (over z, x).
Axes of the slice: x: 2, y: 2, z: 4, core: 2. Of those that a mesh axis runs over, the one named last changes fastest.
Arguments:
- scores: bfloat16 [512, 43008], P('seq', 'blk'), may hold values from 0.09 to 136
- counts: int32 [512], P('seq'), may hold values from 1 to 64
Outputs:
- covariance_tiles: float32 [4, 10752, 43008], P(None, 'seq', 'blk')
All inputs are finite; a program needn't handle non-finite values.
Results may differ from a plain program's by a relative error of at most 0.0023.
Values may be sent and summed in bfloat16 or wider, within the bound.
No kernel may reach another device: no remote copies, remote signals or barrier semaphores. Data moves between devices by JAX's collectives and lax.ppermute only.
A program may use at most 320 MiB of HBM per device.

v0:
```python
import jax
import jax.numpy as jnp
from jax import lax
from jax.sharding import PartitionSpec as P

STATES = 21


def from_behind(value, axis, steps):
    count = lax.axis_size(axis)
    pairs = [(source, (source + steps) % count) for source in range(count)]
    return lax.ppermute(value, axis, pairs)


def partner_stripes(stripe_here):
    rounds_count = min(4, lax.axis_size("blk") - 1)
    received = [stripe_here]
    for shift_by in range(1, rounds_count + 1):
        received.append(from_behind(stripe_here, "blk", shift_by))
    return jnp.stack(received, axis=0)


def body(scores, counts):
    seq_rows = scores.shape[0]
    block_pos = scores.shape[1] // STATES
    raw = scores.astype(jnp.float32).reshape(seq_rows, block_pos, STATES)
    profile = raw / jnp.sum(raw, axis=2, keepdims=True)
    profile = profile.reshape(seq_rows, block_pos * STATES)
    weight = 1.0 / counts.astype(jnp.float32)
    total_weight, frequency = lax.psum(
        (jnp.sum(weight), jnp.sum(weight[:, None] * profile, axis=0)), "seq"
    )
    freq = frequency / total_weight
    scaled = jnp.sqrt(weight * STATES / total_weight)
    centered = (scaled[:, None] * (profile - freq[None, :])).astype(jnp.bfloat16)
    block_cols = centered.shape[1]
    stripe_width = block_cols // lax.axis_size("seq")
    gathered = lax.all_gather(centered, "seq", axis=0, tiled=True)
    seq_index = lax.axis_index("seq")
    stripe_here = lax.dynamic_slice_in_dim(gathered, seq_index * stripe_width, stripe_width, 1)
    partners = partner_stripes(stripe_here)
    covariance = jnp.einsum("kmr,mc->krc", partners, gathered, preferred_element_type=jnp.float32)
    return covariance


def solution(mesh):
    return jax.shard_map(
        body,
        mesh=mesh,
        in_specs=(P("seq", "blk"), P("seq")),
        out_specs=P(None, "seq", "blk"),
        check_vma=False,
    )
```

profile of v0, /device:TPU:0, one launch (start us, length us, event | category | flops | bytes accessed | tf_op | source)
XLA Modules:
  0.0 395.0 jit_solution(13124997728322028905)
XLA Ops:
  6.5 0.0 all-gather.2.cloned.1.call-start
  6.5 1.3 fusion.11
  7.8 4.2 %copy.12 = f32[64,10752]{0,1:T(8,128)} copy(bf16[64,10752]{1,0:T(8,128)(2,1)} %param.2) | data formatting | bytes 4128768 | tf_op jit(solution)/shard_map/convert_element_type | solution.py:26
  12.0 6.8 %reshape.9 = f32[64,512,21]{0,2,1:T(8,128)} reshape(f32[64,10752]{0,1:T(8,128)} %copy.12) | data formatting | bytes 5505024 | tf_op jit(solution)/shard_map/reshape | solution.py:26
  18.8 6.1 %fusion = f32[64,512,21]{0,2,1:T(8,128)} fusion(f32[64,512,21]{0,2,1:T(8,128)} %reshape.9), kind=kOutput, calls=%fused_computation | output fusion | flops 32788 | bytes 5505024 | tf_op jit(solution)/shard_map/div | solution.py:27
  24.9 6.8 %div.34 = f32[64,10752]{0,1:T(8,128)} reshape(f32[64,512,21]{0,2,1:T(8,128)} %fusion) | data formatting | bytes 5505024 | tf_op jit(solution)/shard_map/div | solution.py:27
  31.6 4.1 %copy.13 = f32[64,10752]{1,0:T(8,128)S(1)} copy(f32[64,10752]{0,1:T(8,128)} %div.34) | data formatting | bytes 5505024 | tf_op jit(solution)/shard_map/div | solution.py:27
  35.7 2.0 multiply_reduce_fusion
  37.7 40.3 %all-reduce = (f32[10752]{0:T(1024)S(1)}, f32[]{:T(128)}) all-reduce(f32[10752]{0:T(1024)S(1)} %multiply_reduce_fusion, f32[]{:T(128)} %get-tuple-element.7), channel_id=1, replica_groups=mesh['blk'=4,'seq'=8] {'seq'}, use_global_device_ids=true, to_apply=%region_4.0 | all-reduce | flops 10753 | bytes 86024 | tf_op jit(solution)/shard_map/psum | solution.py:30
  77.9 0.7 divide_sqrt_fusion
  78.6 0.7 broadcast_divide_fusion
  79.3 2.9 multiply_convert_fusion
  82.2 0.0 all-gather.2.cloned.1.call-update
  82.2 154.7 %all-gather.2.cloned.1.call-done = bf16[512,10752]{1,0:T(8,128)(2,1)} async-done(((bf16[64,10752]{1,0:T(8,128)(2,1)}), bf16[512,10752]{1,0:T(8,128)(2,1)}) %all-gather.2.cloned.1.call-update) | async-done | bytes 11010064 | tf_op jit(solution)/shard_map/all_gather | solution.py:38
  236.9 2.3 constant_dynamic-slice_fusion
  239.2 0.7 copy.14
  239.9 0.6 collective-permute-start.2
  240.5 1.0 collective-permute-start.1
  241.5 0.2 collective-permute-start
  241.7 28.9 %collective-permute-done.2 = bf16[512,1344]{0,1:T(8,128)(2,1)S(1)} collective-permute-done((bf16[512,1344]{0,1:T(8,128)(2,1)S(1)}, bf16[512,1344]{0,1:T(8,128)(2,1)S(1)}, u32[]{:S(2)}, u32[]{:S(2)}) %collective-permute-start.2) | collective-permute-done | bytes 1376288 | tf_op jit(solution)/shard_map/ppermute | solution.py:12
  270.6 31.3 %collective-permute-done.1 = bf16[512,1344]{0,1:T(8,128)(2,1)S(1)} collective-permute-done((bf16[512,1344]{0,1:T(8,128)(2,1)S(1)}, bf16[512,1344]{0,1:T(8,128)(2,1)S(1)}, u32[]{:S(2)}, u32[]{:S(2)}) %collective-permute-start.1) | collective-permute-done | bytes 1376288 | tf_op jit(solution)/shard_map/ppermute | solution.py:12
  301.9 0.0 copy-start
  301.9 0.1 collective-permute-done
  302.0 1.0 copy-done
  302.9 0.0 copy-start.1
  302.9 1.1 copy-done.1
  304.1 84.0 %fusion.1 = f32[4,1344,10752]{2,1,0:T(8,128)} fusion(bf16[512,10752]{1,0:T(8,128)(2,1)} %all-gather.2.cloned.1.call-done, bf16[1,512,1344]{1,2,0:T(8,128)(2,1)S(1)} %bitcast.14, bf16[1,512,1344]{1,2,0:T(8,128)(2,1)} %bitcast.15, bf16[1,512,1344]{1,2,0:T(8,128)(2,1)} %bitcast.16, bf16[1,512,1344]{1,2,0:T(8,128)(2,1)S(1)} %bitcast.13), kind=kOutput, calls=%fused_computation.1 | convolution fusion | flops 59198275584 | bytes 247726080 | tf_op jit(solution)/shard_map/kmr,mc->krc/dot_general | solution.py:42
Async XLA Ops:
  6.5 230.4 %all-gather.2.cloned.1.call-start = ((), (), s32[]{:S(2)}) async-start(), calls=%async_computation | async-start | bytes 12386304 | tf_op jit(solution)/shard_map/all_gather | solution.py:38
  239.9 30.7 %collective-permute-start.2 = (bf16[512,1344]{0,1:T(8,128)(2,1)S(1)}, bf16[512,1344]{0,1:T(8,128)(2,1)S(1)}, u32[]{:S(2)}, u32[]{:S(2)}) collective-permute-start(bf16[512,1344]{0,1:T(8,128)(2,1)S(1)} %copy.14), channel_id=1, source_target_pairs={{0,24},{8,0},{16,8},{24,16},{1,25},{9,1},{17,9},{25,17},{2,26},{10... | collective-permute-start | bytes 4128776 | tf_op jit(solution)/shard_map/ppermute | solution.py:12
  240.5 61.4 %collective-permute-start.1 = (bf16[512,1344]{0,1:T(8,128)(2,1)S(1)}, bf16[512,1344]{0,1:T(8,128)(2,1)S(1)}, u32[]{:S(2)}, u32[]{:S(2)}) collective-permute-start(bf16[512,1344]{0,1:T(8,128)(2,1)S(1)} %copy.14), channel_id=1, source_target_pairs={{0,16},{8,24},{16,0},{24,8},{1,17},{9,25},{17,1},{25,9},{2,18},{10... | collective-permute-start | bytes 4128776 | tf_op jit(solution)/shard_map/ppermute | solution.py:12
  241.5 60.4 %collective-permute-start = (bf16[512,1344]{0,1:T(8,128)(2,1)S(1)}, bf16[512,1344]{0,1:T(8,128)(2,1)S(1)}, u32[]{:S(2)}, u32[]{:S(2)}) collective-permute-start(bf16[512,1344]{0,1:T(8,128)(2,1)S(1)} %copy.14), channel_id=1, source_target_pairs={{0,8},{8,16},{16,24},{24,0},{1,9},{9,17},{17,25},{25,1},{2,10},{10... | collective-permute-start | bytes 4128776 | tf_op jit(solution)/shard_map/ppermute | solution.py:12
  301.9 1.1 copy-start
  302.9 1.2 copy-start.1
Sparse Core Ops, SparseCore 0:
  82.4 154.5 all-gather.1
where the time goes:
time: 396 us; the launch traced here: 395 us
  waiting for transfers between devices  215 us (54%)
  matrix products  84 us (21%)
  blocking collectives  40.3 us (10%)
  local copies, waits for them, and re-layouts  26.9 us (7%)
  other arithmetic  13.5 us (3%)
  between operations  13.4 us (3%)
    all_gather x1, waiting for transfers between devices, body(): gathered = lax.all_gather(centered, 'seq', axis=0, tiled=True)  155 us
    dot_general x1, matrix products, body(): jnp.einsum('kmr,mc->krc', partners, gathered, preferred_element_type=jnp....  84 us
    ppermute x3, waiting for transfers between devices, from_behind(): return lax.ppermute(value, axis, pairs)  60.3 us
    psum x1, blocking collectives, body(): lax.psum((jnp.sum(weight), jnp.sum(weight[:, None] * profile, axis=0)), '...  40.3 us
    div x2, local copies, waits for them, and re-layouts, body(): profile = raw / jnp.sum(raw, axis=2, keepdims=True)  10.8 us
  transfers between devices with their start and end apart: 4, of which 4 were waited for; matrix products, arithmetic and copies ran while one was open for 0% of the time, Pallas kernels for 0%

commit v1 on v0

--- a/solution.py
+++ b/solution.py
@@ -1,9 +1,15 @@
+import functools
+
 import jax
 import jax.numpy as jnp
 from jax import lax
+from jax.experimental import pallas as pl
+from jax.experimental.pallas import tpu as pltpu
 from jax.sharding import PartitionSpec as P
 
 STATES = 21
+LANE = 128
+VMEM_LIMIT = 56 * 2**20
 
 
 def from_behind(value, axis, steps):
@@ -20,7 +26,7 @@
     return jnp.stack(received, axis=0)
 
 
-def body(scores, counts):
+def plain_body(scores, counts):
     seq_rows = scores.shape[0]
     block_pos = scores.shape[1] // STATES
     raw = scores.astype(jnp.float32).reshape(seq_rows, block_pos, STATES)
@@ -39,11 +45,235 @@
     seq_index = lax.axis_index("seq")
     stripe_here = lax.dynamic_slice_in_dim(gathered, seq_index * stripe_width, stripe_width, 1)
     partners = partner_stripes(stripe_here)
-    covariance = jnp.einsum("kmr,mc->krc", partners, gathered, preferred_element_type=jnp.float32)
-    return covariance
+    return jnp.einsum("kmr,mc->krc", partners, gathered, preferred_element_type=jnp.float32)
+
+
+def center_kernel(raw_ref, weight_ref, out_ref):
+    seqs, width = raw_ref.shape
+    pos = width // STATES
+    raw = raw_ref[...]
+    first = STATES * lax.broadcasted_iota(jnp.int32, (pos, width), 0)
+    here = lax.broadcasted_iota(jnp.int32, (pos, width), 1)
+    member = ((here >= first) & (here < first + STATES)).astype(jnp.bfloat16)
+    sums = lax.dot_general(
+        raw, member, (((1,), (1,)), ((), ())), preferred_element_type=jnp.float32
+    )
+    high = sums.astype(jnp.bfloat16)
+    rest = sums - high.astype(jnp.float32)
+    mid = rest.astype(jnp.bfloat16)
+    low = (rest - mid.astype(jnp.float32)).astype(jnp.bfloat16)
+    spread = (
+        jnp.dot(high, member, preferred_element_type=jnp.float32)
+        + jnp.dot(mid, member, preferred_element_type=jnp.float32)
+    ) + jnp.dot(low, member, preferred_element_type=jnp.float32)
+    profile = raw.astype(jnp.float32) / spread
+    weight = weight_ref[...]
+    total = jnp.sum(weight, axis=0, keepdims=True)
+    freq = jnp.sum(weight * profile, axis=0, keepdims=True) / total
+    scaled = jnp.sqrt(weight * STATES / total)
+    centered = (scaled * (profile - freq)).astype(jnp.bfloat16)
+    out_ref[...] = centered.T
+
+
+def center(raw, weight):
+    seqs, width = raw.shape
+    vmem = pl.BlockSpec(memory_space=pltpu.VMEM)
+    return pl.pallas_call(
+        center_kernel,
+        out_shape=jax.ShapeDtypeStruct((width, seqs), jnp.bfloat16),
+        in_specs=[vmem, vmem],
+        out_specs=vmem,
+        compiler_params=pltpu.CompilerParams(vmem_limit_bytes=VMEM_LIMIT),
+        name="center",
+    )(raw, weight.reshape(seqs, 1))
+
+
+def tiles_kernel(lefts, sizes, tall, split, where, *refs):
+    left, refs = refs[:lefts], refs[lefts:]
+    pieces, refs = refs[: len(sizes)], refs[len(sizes) :]
+    out, left_buf, right, out_buf, left_sem, right_sem, out_sem = refs[-7:]
+    stripe = left[0].shape[0]
+    width = right.shape[0]
+    per = stripe // tall
+    steps = lefts * per
+    small = tall // split
+    column = pl.multiple_of(where[0] * LANE, LANE)
+    rounds = 1 + 2 * len(sizes)
+
+    def load(step, act):
+        which = step // per
+        row = pl.multiple_of(lax.rem(step, per) * tall, 16)
+        slot = lax.rem(step, 2)
+        for j in range(lefts):
+
+            @pl.when(which == j)
+            def _():
+                act(pltpu.make_async_copy(
+                    left[j].at[pl.ds(row, tall)], left_buf.at[slot], left_sem.at[slot]
+                ))
+
+    def store(step, j):
+        row = pl.multiple_of(lax.rem(step, per) * tall, 8)
+        slot = lax.rem(step, 2)
+        return pltpu.make_async_copy(
+            out_buf.at[slot, pl.ds(j * small, small)],
+            out.at[where[rounds + step // per], pl.ds(row + j * small, small), pl.ds(column, width)],
+            out_sem.at[slot, j],
+        )
+
+    gather = [
+        pltpu.make_async_copy(
+            pieces[i].at[pl.ds(pl.multiple_of(where[1 + 2 * i], 16), size)],
+            right.at[pl.ds(pl.multiple_of(where[2 + 2 * i], 16), size)],
+            right_sem.at[i],
+        )
+        for i, size in enumerate(sizes)
+    ]
+    load(0, lambda copy: copy.start())
+    for copy in gather:
+        copy.start()
+    for copy in gather:
+        copy.wait()
+
+    def body(step, _):
+        slot = lax.rem(step, 2)
+
+        @pl.when(step + 1 < steps)
+        def _():
+            load(step + 1, lambda copy: copy.start())
+
+        load(step, lambda copy: copy.wait())
+        for j in range(split):
+
+            @pl.when(step >= 2)
+            def _():
+                store(step - 2, j).wait()
+
+            out_buf[slot, j * small : (j + 1) * small, :] = lax.dot_general(
+                left_buf[slot, j * small : (j + 1) * small, :],
+                right[...],
+                (((1,), (1,)), ((), ())),
+                preferred_element_type=jnp.float32,
+            )
+            store(step, j).start()
+        return 0
+
+    lax.fori_loop(0, steps, body, 0)
+    for step in (steps - 2, steps - 1):
+        for j in range(split):
+            store(step, j).wait()
+
+
+def tiles(out, out_shape, column, left, rounds, pieces, width, tall=672, split=2):
+    stripe, depth = left[0].shape
+    sizes = tuple(size for _, _, size, _ in pieces)
+    where = [column]
+    for _, source, _, target in pieces:
+        where += [source, target]
+    where = jnp.stack([jnp.asarray(v, jnp.int32) for v in where + list(rounds)])
+    anywhere = pl.BlockSpec(memory_space=pl.ANY)
+    operands = [where, *left, *(piece[0] for piece in pieces)]
+    specs = [pl.BlockSpec(memory_space=pltpu.SMEM)] + [anywhere] * (len(operands) - 1)
+    aliases = {}
+    if out is not None:
+        aliases = {len(operands): 0}
+        operands.append(out)
+        specs.append(anywhere)
+    return pl.pallas_call(
+        functools.partial(tiles_kernel, len(left), sizes, tall, split),
+        out_shape=jax.ShapeDtypeStruct(out_shape, jnp.float32),
+        in_specs=specs,
+        out_specs=anywhere,
+        scratch_shapes=[
+            pltpu.VMEM((2, tall, depth), jnp.bfloat16),
+            pltpu.VMEM((width, depth), jnp.bfloat16),
+            pltpu.VMEM((2, tall, width), jnp.float32),
+            pltpu.SemaphoreType.DMA((2,)),
+            pltpu.SemaphoreType.DMA((len(sizes),)),
+            pltpu.SemaphoreType.DMA((2, split)),
+        ],
+        input_output_aliases=aliases,
+        compiler_params=pltpu.CompilerParams(vmem_limit_bytes=VMEM_LIMIT),
+        cost_estimate=pl.CostEstimate(
+            flops=2 * len(left) * stripe * width * depth,
+            bytes_accessed=4 * len(left) * stripe * width,
+            transcendentals=0,
+        ),
+        name="tiles",
+    )(*operands)
+
+
+def flip(value, axis, bits):
+    count = lax.axis_size(axis)
+    return lax.ppermute(value, axis, [(source, source ^ bits) for source in range(count)])
+
+
+def wait_all(*values):
+    return lax.optimization_barrier(values)
+
+
+def fast_body(scores, counts):
+    blocks, seqs_axis = lax.axis_size("blk"), lax.axis_size("seq")
+    stripe = scores.shape[1] // seqs_axis
+    out_shape = (blocks, stripe, scores.shape[1])
+    raw = lax.all_to_all(scores, "seq", 1, 0, tiled=True)
+    all_counts = lax.all_gather(counts, "seq", axis=0, tiled=True)
+    weight = 1.0 / all_counts.astype(jnp.float32)
+    own = center(raw, weight)
+
+    seq, blk = lax.axis_index("seq"), lax.axis_index("blk")
+    x, z, core = seq % 2, seq // 2, blk % 2
+    middle = (z == 1) | (z == 2)
+    rounds = [0, 2, 3 - 2 * core, 1 + 2 * core]
+    pair_tiles = 2 * stripe // LANE
+
+    def pair(out, flipped, mine, others, left, rounds):
+        pieces = [(mine, 0, stripe, x * stripe)]
+        row = (1 - x) * stripe
+        for other in others:
+            pieces.append((other, 0, other.shape[0], row))
+            row = row + other.shape[0]
+        column = (z ^ flipped) * pair_tiles
+        return tiles(out, out_shape, column, left, rounds, pieces, 2 * stripe)
+
+    x_own = flip(own, "seq", 1)
+    z1 = flip(own, "seq", 2)
+    z3_middle = lax.ppermute(own, "seq", [(2, 4), (4, 2), (3, 5), (5, 3)])
+    y_own = flip(own, "blk", 2)
+    core_own = flip(own, "blk", 1)
+    own, x_own, z1, z3_middle, y_own, core_own = wait_all(
+        own, x_own, z1, z3_middle, y_own, core_own
+    )
+    core_y = flip(y_own, "blk", 1)
+    x_z1 = flip(z1, "seq", 1)
+    z3_outer = lax.ppermute(own, "seq", [(0, 6), (6, 0), (1, 7), (7, 1)])
+    left = [own, y_own, core_own, core_y]
+    out = pair(None, 0, own, [x_own], left, rounds)
+    out, x_z1, z3_outer = wait_all(out, x_z1, z3_outer)
+    z3 = jnp.where(middle, z3_middle, z3_outer)
+    x_z3 = flip(z3, "seq", 1)
+    z2 = flip(z3, "seq", 2)
+    out = pair(out, 1, z1, [x_z1], left, rounds)
+    out, x_z3, z2 = wait_all(out, x_z3, z2)
+    half = stripe // 2
+    x_z2 = [flip(z2[:half], "seq", 1), flip(x_z3[half:], "seq", 2)]
+    out = pair(out, 3, z3, [x_z3], left, rounds)
+    out = pair(out, 2, z2, x_z2, left, rounds)
+    return out
 
 
 def solution(mesh):
+    def body(scores, counts):
+        stripe_width = scores.shape[1] // mesh.shape["seq"]
+        fits = (
+            mesh.shape["blk"] == 4
+            and mesh.shape["seq"] == 8
+            and stripe_width % 64 == 0
+            and stripe_width % STATES == 0
+            and stripe_width % 672 == 0
+        )
+        return (fast_body if fits else plain_body)(scores, counts)
+
     return jax.shard_map(
         body,
         mesh=mesh,

time: 396 us -> 217 us (0.55)
  waiting for transfers between devices: 215 us -> 43.3 us
  Pallas kernels: 0 us -> 105 us
  matrix products: 84 us -> 0 us
  starting transfers between devices: 1.77 us -> 20.9 us
  other arithmetic: 13.5 us -> 0.15 us
  local copies, waits for them, and re-layouts: 26.9 us -> 13.6 us
  between operations: 13.4 us -> 0.93 us
  blocking collectives: 40.3 us -> 32.9 us
    all_gather x1 -> x0, waiting for transfers between devices: 155 us -> none  [body(): gathered = lax.all_gather(centered, 'seq', axis=0, tiled=True)]
    pallas_call x0 -> x5, Pallas kernels: none -> 105 us  [the longest x4 99.6 us: tiles(): pl.pallas_call(functools.partial(tiles_kernel, len(left), sizes, tall, sp...]
    dot_general x1 -> x0, matrix products: 84 us -> none  [body(): jnp.einsum('kmr,mc->krc', partners, gathered, preferred_element_type=jnp....]
    psum x1 -> x0, blocking collectives: 40.3 us -> none  [body(): lax.psum((jnp.sum(weight), jnp.sum(weight[:, None] * profile, axis=0)), '...]
    unnamed x0 -> x1, blocking collectives: none -> 32.9 us
    ppermute x3 -> x12, waiting for transfers between devices: 60.3 us -> 43.3 us  [the longest x10 38.5 us: flip(): lax.ppermute(value, axis, [(source, source ^ bits) for source in range(co...]
    ppermute x3 -> x12, starting transfers between devices: 1.77 us -> 13.5 us  [the longest x10 9.23 us: flip(): lax.ppermute(value, axis, [(source, source ^ bits) for source in range(co...]
    div x2 -> x0, local copies, waits for them, and re-layouts: 10.8 us -> none  [body(): profile = raw / jnp.sum(raw, axis=2, keepdims=True)]
  transfers between devices with their start and end apart: 4 -> 13, of which waited for: 4 -> 6; matrix products, arithmetic and copies ran while one was open for 0% -> 2% of each run, Pallas kernels for 0% -> 34%
where the time goes in v1:
time: 217 us
  Pallas kernels  105 us (48%)
  waiting for transfers between devices  43.3 us (20%)
  blocking collectives  32.9 us (15%)
  starting transfers between devices  20.9 us (10%)
  local copies, waits for them, and re-layouts  13.6 us (6%)
    pallas_call x4, Pallas kernels, tiles(): pl.pallas_call(functools.partial(tiles_kernel, len(left), sizes, tall, sp...  99.6 us
    ppermute x10, waiting for transfers between devices, flip(): lax.ppermute(value, axis, [(source, source ^ bits) for source in range(co...  38.5 us
    unnamed x1, blocking collectives  32.9 us
    ppermute x10, starting transfers between devices, flip(): lax.ppermute(value, axis, [(source, source ^ bits) for source in range(co...  9.23 us
    all_to_all x1, starting transfers between devices, fast_body(): raw = lax.all_to_all(scores, 'seq', 1, 0, tiled=True)  7.38 us
    unnamed x33, local copies, waits for them, and re-layouts  5.99 us
    pallas_call x1, Pallas kernels, center(): pl.pallas_call(center_kernel, out_shape=jax.ShapeDtypeStruct((width, seqs...  5.25 us
    ppermute x1, waiting for transfers between devices, fast_body(): z3_outer = lax.ppermute(own, 'seq', [(0, 6), (6, 0), (1, 7), (7, 1)])  4.82 us
  transfers between devices with their start and end apart: 13, of which 6 were waited for; matrix products, arithmetic and copies ran while one was open for 2% of the time, Pallas kernels for 34%

profile of v1, /device:TPU:0, one launch (start us, length us, event | category | flops | bytes accessed | tf_op | source)
XLA Modules:
  0.0 216.7 jit_solution(15504133610200197000)
XLA Ops:
  0.0 2.9 %all_to_all.14 = bf16[64,8,1344]{2,1,0:T(8,128)(2,1)S(1)} reshape(bf16[64,10752]{1,0:T(8,128)(2,1)} %param.2) | data formatting | bytes 2752512 | tf_op jit(solution)/shard_map/all_to_all | solution.py:219
  2.9 1.3 copy.7
  4.2 7.4 %all-to-all-start = ((bf16[64,8,1344]{2,0,1:T(8,128)(2,1)}), bf16[64,8,1344]{2,0,1:T(8,128)(2,1)S(1)}, u32[]{:S(2)}, u32[]{:S(2)}) async-start(bf16[64,8,1344]{2,0,1:T(8,128)(2,1)} %copy.7), calls=%async_computation | async-start | bytes 2883584 | tf_op jit(solution)/shard_map/all_to_all | solution.py:219
  13.0 32.9 %all-reduce = s32[512]{0:T(512)S(1)} all-reduce(s32[512]{0:T(512)S(1)} %dynamic-update-slice), channel_id=1, replica_groups=mesh['blk'=4,'seq'=8] {'seq'}, use_global_device_ids=true, to_apply=%add | all-reduce | flops 512 | bytes 4096
  45.9 0.9 copy.8.weight_ref
  46.8 1.1 copy-done.2
  47.9 5.3 %center.1.refs_0_.refs_4_ = bf16[1344,512]{1,0:T(8,128)(2,1)} custom-call(bf16[512,1344]{1,0:T(8,128)(2,1)} %bitcast.14, f32[512,1]{1,0:T(8,128)} %copy.8.weight_ref), custom_call_target="tpu_custom_call" | custom-call | tf_op jit(solution)/shard_map/center/pallas_call | solution.py:81
  53.2 1.5 collective-permute-start.3
  54.7 0.7 collective-permute-start.2
  55.4 1.4 collective-permute-start.1
  56.8 1.4 collective-permute-start
  58.2 27.7 %collective-permute-done.3.refs_1_ = bf16[1344,512]{1,0:T(8,128)(2,1)S(1)} collective-permute-done((bf16[1344,512]{1,0:T(8,128)(2,1)}, bf16[1344,512]{1,0:T(8,128)(2,1)S(1)}, u32[]{:S(2)}, u32[]{:S(2)}) %collective-permute-start.3) | collective-permute-done | bytes 1376288 | tf_op jit(solution)/shard_map/ppermute | solution.py:208
  86.0 2.0 collective-permute-done.1.refs_4_
  88.0 1.1 copy-done.6
  89.1 1.2 copy-done.7
  90.3 0.6 stack.59.where
  90.9 0.7 stack.61.where
  92.2 0.6 stack.57.where
  92.8 1.4 collective-permute-start.6
  94.2 3.6 %collective-permute-start.7 = (bf16[1344,512]{1,0:T(8,128)(2,1)}, bf16[1344,512]{1,0:T(8,128)(2,1)S(1)}, u32[]{:S(2)}, u32[]{:S(2)}) collective-permute-start(bf16[1344,512]{1,0:T(8,128)(2,1)} %center.1.refs_0_.refs_4_), channel_id=1, source_target_pairs={{0,6},{6,0},{1,7},{7,1},{8,14},{14,8},{9,15},{15,9},{16,22},{22,16... | collective-permute-start | bytes 4128776 | tf_op jit(solution)/shard_map/ppermute | solution.py:249
  97.9 24.9 %tiles.4.refs_6_ = f32[4,1344,10752]{2,1,0:T(8,128)} custom-call(s32[9]{0:T(128)} %stack.61.where, bf16[1344,512]{1,0:T(8,128)(2,1)} %center.1.refs_0_.refs_4_, bf16[1344,512]{1,0:T(8,128)(2,1)} %copy-done.1, bf16[1344,512]{1,0:T(8,128)(2,1)} %copy-done, bf16[1344,512]{1,0:T(8,128)(2,1)} %collective-permute-done.5.refs_3_, ...), custom_call_target="tpu_custom_call" | custom-call | flops 14797504512 | bytes 57802752 | tf_op jit(solution)/shard_map/tiles/pallas_call | solution.py:182
  122.8 2.8 %collective-permute-done.6.refs_5_ = bf16[1344,512]{1,0:T(8,128)(2,1)S(1)} collective-permute-done((bf16[1344,512]{1,0:T(8,128)(2,1)}, bf16[1344,512]{1,0:T(8,128)(2,1)S(1)}, u32[]{:S(2)}, u32[]{:S(2)}) %collective-permute-start.6) | collective-permute-done | bytes 1376288 | tf_op jit(solution)/shard_map/ppermute | solution.py:208
  125.6 4.8 %collective-permute-done.7 = bf16[1344,512]{1,0:T(8,128)(2,1)S(1)} collective-permute-done((bf16[1344,512]{1,0:T(8,128)(2,1)}, bf16[1344,512]{1,0:T(8,128)(2,1)S(1)}, u32[]{:S(2)}, u32[]{:S(2)}) %collective-permute-start.7) | collective-permute-done | bytes 1376288 | tf_op jit(solution)/shard_map/ppermute | solution.py:249
  130.7 0.8 collective-permute-start.8
  131.5 24.9 %tiles.5.refs_6_ = f32[4,1344,10752]{2,1,0:T(8,128)} custom-call(s32[9]{0:T(128)} %stack.59.where, bf16[1344,512]{1,0:T(8,128)(2,1)} %center.1.refs_0_.refs_4_, bf16[1344,512]{1,0:T(8,128)(2,1)} %copy-done.1, bf16[1344,512]{1,0:T(8,128)(2,1)} %copy-done, bf16[1344,512]{1,0:T(8,128)(2,1)} %collective-permute-done.5.refs_3_, ...), custom_call_target="tpu_custom_call", output_to_operand_aliasing={{}: (7, {})} | custom-call | flops 14797504512 | bytes 57802752 | tf_op jit(solution)/shard_map/tiles/pallas_call | solution.py:182
  156.4 5.8 %collective-permute-done.9.refs_4_ = bf16[1344,512]{1,0:T(8,128)(2,1)S(1)} collective-permute-done((bf16[1344,512]{1,0:T(8,128)(2,1)S(1)}, bf16[1344,512]{1,0:T(8,128)(2,1)S(1)}, u32[]{:S(2)}, u32[]{:S(2)}) %collective-permute-start.9) | collective-permute-done | bytes 1376288 | tf_op jit(solution)/shard_map/ppermute | solution.py:208
  162.3 0.9 collective-permute-start.10
  163.3 1.7 collective-permute-start.11
  164.9 24.9 %tiles.6.refs_7_ = f32[4,1344,10752]{2,1,0:T(8,128)} custom-call(s32[9]{0:T(128)} %stack.63.where, bf16[1344,512]{1,0:T(8,128)(2,1)} %center.1.refs_0_.refs_4_, bf16[1344,512]{1,0:T(8,128)(2,1)} %copy-done.1, bf16[1344,512]{1,0:T(8,128)(2,1)} %copy-done, bf16[1344,512]{1,0:T(8,128)(2,1)} %collective-permute-done.5.refs_3_, ...), custom_call_target="tpu_custom_call", output_to_operand_aliasing={{}: (7, {})} | custom-call | flops 14797504512 | bytes 57802752 | tf_op jit(solution)/shard_map/tiles/pallas_call | solution.py:182
  189.9 0.8 copy-done.11
  190.7 0.9 copy-done.12
  191.6 24.9 %tiles.7 = f32[4,1344,10752]{2,1,0:T(8,128)} custom-call(s32[11]{0:T(128)} %stack.57.where, bf16[1344,512]{1,0:T(8,128)(2,1)} %center.1.refs_0_.refs_4_, bf16[1344,512]{1,0:T(8,128)(2,1)} %copy-done.1, bf16[1344,512]{1,0:T(8,128)(2,1)} %copy-done, bf16[1344,512]{1,0:T(8,128)(2,1)} %collective-permute-done.5.refs_3_, ...), custom_call_target="tpu_custom_call", output_to_operand_aliasing={{}: (8, {})} | custom-call | flops 14797504512 | bytes 57802752 | tf_op jit(solution)/shard_map/tiles/pallas_call | solution.py:182
  (44 shorter events, 1.9 us)
Async XLA Ops:
  4.2 7.4 %copy-start.14 = (u32[32]{0:T(128)S(1)}, u32[32]{0:T(128)}, u32[]{:S(2)}) copy-start(u32[32]{0:T(128)} %constant.53) | copy-start | bytes 388
  4.2 8.6 %copy-start.13 = (s32[64]{0:T(128)S(1)}, s32[64]{0:T(128)}, u32[]{:S(2)}) copy-start(s32[64]{0:T(128)} %param.3) | copy-start | bytes 772
  4.2 42.7 %all-to-all-start = ((bf16[64,8,1344]{2,0,1:T(8,128)(2,1)}), bf16[64,8,1344]{2,0,1:T(8,128)(2,1)S(1)}, u32[]{:S(2)}, u32[]{:S(2)}) async-start(bf16[64,8,1344]{2,0,1:T(8,128)(2,1)} %copy.7), calls=%async_computation | async-start | bytes 2883584 | tf_op jit(solution)/shard_map/all_to_all | solution.py:219
  46.8 1.1 copy-start.2
  53.2 5.1 %collective-permute-start.4 = (bf16[1344,512]{1,0:T(8,128)(2,1)}, bf16[1344,512]{1,0:T(8,128)(2,1)S(1)}, u32[]{:S(2)}, u32[]{:S(2)}) collective-permute-start(bf16[1344,512]{1,0:T(8,128)(2,1)} %center.1.refs_0_.refs_4_), channel_id=1, source_target_pairs={{0,8},{8,0},{16,24},{24,16},{1,9},{9,1},{17,25},{25,17},{2,10},{10... | collective-permute-start | bytes 4128776 | tf_op jit(solution)/shard_map/ppermute | solution.py:208
  53.2 32.8 %collective-permute-start.3 = (bf16[1344,512]{1,0:T(8,128)(2,1)}, bf16[1344,512]{1,0:T(8,128)(2,1)S(1)}, u32[]{:S(2)}, u32[]{:S(2)}) collective-permute-start(bf16[1344,512]{1,0:T(8,128)(2,1)} %center.1.refs_0_.refs_4_), channel_id=1, source_target_pairs={{0,16},{8,24},{16,0},{24,8},{1,17},{9,25},{17,1},{25,9},{2,18},{10... | collective-permute-start | bytes 4128776 | tf_op jit(solution)/shard_map/ppermute | solution.py:208
  54.7 31.3 %collective-permute-start.2 = (bf16[1344,512]{1,0:T(8,128)(2,1)}, bf16[1344,512]{1,0:T(8,128)(2,1)S(1)}, u32[]{:S(2)}, u32[]{:S(2)}) collective-permute-start(bf16[1344,512]{1,0:T(8,128)(2,1)} %center.1.refs_0_.refs_4_), channel_id=1, source_target_pairs={{2,4},{4,2},{3,5},{5,3},{10,12},{12,10},{11,13},{13,11},{18,20},{2... | collective-permute-start | bytes 4128776 | tf_op jit(solution)/shard_map/ppermute | solution.py:241
  55.4 32.6 %collective-permute-start.1 = (bf16[1344,512]{1,0:T(8,128)(2,1)}, bf16[1344,512]{1,0:T(8,128)(2,1)S(1)}, u32[]{:S(2)}, u32[]{:S(2)}) collective-permute-start(bf16[1344,512]{1,0:T(8,128)(2,1)} %center.1.refs_0_.refs_4_), channel_id=1, source_target_pairs={{0,2},{1,3},{2,0},{3,1},{4,6},{5,7},{6,4},{7,5},{8,10},{9,11},{10,... | collective-permute-start | bytes 4128776 | tf_op jit(solution)/shard_map/ppermute | solution.py:208
  56.8 32.3 %collective-permute-start = (bf16[1344,512]{1,0:T(8,128)(2,1)}, bf16[1344,512]{1,0:T(8,128)(2,1)S(1)}, u32[]{:S(2)}, u32[]{:S(2)}) collective-permute-start(bf16[1344,512]{1,0:T(8,128)(2,1)} %center.1.refs_0_.refs_4_), channel_id=1, source_target_pairs={{0,1},{1,0},{2,3},{3,2},{4,5},{5,4},{6,7},{7,6},{8,9},{9,8},{10,11... | collective-permute-start | bytes 4128776 | tf_op jit(solution)/shard_map/ppermute | solution.py:208
  58.2 39.6 %copy-start = (bf16[1344,512]{1,0:T(8,128)(2,1)}, bf16[1344,512]{1,0:T(8,128)(2,1)S(1)}, u32[]{:S(2)}) copy-start(bf16[1344,512]{1,0:T(8,128)(2,1)S(1)} %collective-permute-done.4.refs_2_) | copy-start | bytes 4128772
  86.0 11.9 %copy-start.1 = (bf16[1344,512]{1,0:T(8,128)(2,1)}, bf16[1344,512]{1,0:T(8,128)(2,1)S(1)}, u32[]{:S(2)}) copy-start(bf16[1344,512]{1,0:T(8,128)(2,1)S(1)} %collective-permute-done.3.refs_1_) | copy-start | bytes 4128772
  86.0 3.2 %copy-start.9 = (bf16[1344,512]{1,0:T(8,128)(2,1)}, bf16[1344,512]{1,0:T(8,128)(2,1)S(1)}, u32[]{:S(2)}) copy-start(bf16[1344,512]{1,0:T(8,128)(2,1)S(1)} %collective-permute-done.2) | copy-start | bytes 4128772
  88.0 1.1 copy-start.6
  89.1 1.2 copy-start.7
  90.3 7.5 %collective-permute-start.5 = (bf16[1344,512]{1,0:T(8,128)(2,1)S(1)}, bf16[1344,512]{1,0:T(8,128)(2,1)}, u32[]{:S(2)}, u32[]{:S(2)}) collective-permute-start(bf16[1344,512]{1,0:T(8,128)(2,1)S(1)} %collective-permute-done.3.refs_1_), channel_id=1, source_target_pairs={{0,8},{8,0},{16,24},{24,16},{1,9},{9,1},{17,25},{25,17},{2,10},{10... | collective-permute-start | bytes 4128776 | tf_op jit(solution)/shard_map/ppermute | solution.py:208
  92.8 37.6 %copy-start.10 = (bf16[1344,512]{1,0:T(8,128)(2,1)S(1)}, bf16[1344,512]{1,0:T(8,128)(2,1)}, u32[]{:S(2)}) copy-start(bf16[1344,512]{1,0:T(8,128)(2,1)} %copy-done.9) | copy-start | bytes 4128772
  92.8 32.8 %collective-permute-start.6 = (bf16[1344,512]{1,0:T(8,128)(2,1)}, bf16[1344,512]{1,0:T(8,128)(2,1)S(1)}, u32[]{:S(2)}, u32[]{:S(2)}) collective-permute-start(bf16[1344,512]{1,0:T(8,128)(2,1)} %copy-done.6), channel_id=1, source_target_pairs={{0,1},{1,0},{2,3},{3,2},{4,5},{5,4},{6,7},{7,6},{8,9},{9,8},{10,11... | collective-permute-start | bytes 4128776 | tf_op jit(solution)/shard_map/ppermute | solution.py:208
  94.2 36.2 %collective-permute-start.7 = (bf16[1344,512]{1,0:T(8,128)(2,1)}, bf16[1344,512]{1,0:T(8,128)(2,1)S(1)}, u32[]{:S(2)}, u32[]{:S(2)}) collective-permute-start(bf16[1344,512]{1,0:T(8,128)(2,1)} %center.1.refs_0_.refs_4_), channel_id=1, source_target_pairs={{0,6},{6,0},{1,7},{7,1},{8,14},{14,8},{9,15},{15,9},{16,22},{22,16... | collective-permute-start | bytes 4128776 | tf_op jit(solution)/shard_map/ppermute | solution.py:249
  125.6 5.0 %copy-start.8 = (bf16[1344,512]{1,0:T(8,128)(2,1)}, bf16[1344,512]{1,0:T(8,128)(2,1)S(1)}, u32[]{:S(2)}) copy-start(bf16[1344,512]{1,0:T(8,128)(2,1)S(1)} %collective-permute-done.6.refs_5_) | copy-start | bytes 4128772
  130.6 25.8 %copy-start.3 = (bf16[1344,512]{1,0:T(8,128)(2,1)}, bf16[1344,512]{1,0:T(8,128)(2,1)S(1)}, u32[]{:S(2)}) copy-start(bf16[1344,512]{1,0:T(8,128)(2,1)S(1)} %broadcast_select_fusion.refs_4_) | copy-start | bytes 4128772
  130.6 31.6 %collective-permute-start.9 = (bf16[1344,512]{1,0:T(8,128)(2,1)S(1)}, bf16[1344,512]{1,0:T(8,128)(2,1)S(1)}, u32[]{:S(2)}, u32[]{:S(2)}) collective-permute-start(bf16[1344,512]{1,0:T(8,128)(2,1)S(1)} %broadcast_select_fusion.refs_4_), channel_id=1, source_target_pairs={{0,2},{1,3},{2,0},{3,1},{4,6},{5,7},{6,4},{7,5},{8,10},{9,11},{10,... | collective-permute-start | bytes 4128776 | tf_op jit(solution)/shard_map/ppermute | solution.py:208
  130.7 31.6 %collective-permute-start.8 = (bf16[1344,512]{1,0:T(8,128)(2,1)S(1)}, bf16[1344,512]{1,0:T(8,128)(2,1)S(1)}, u32[]{:S(2)}, u32[]{:S(2)}) collective-permute-start(bf16[1344,512]{1,0:T(8,128)(2,1)S(1)} %broadcast_select_fusion.refs_4_), channel_id=1, source_target_pairs={{0,1},{1,0},{2,3},{3,2},{4,5},{5,4},{6,7},{7,6},{8,9},{9,8},{10,11... | collective-permute-start | bytes 4128776 | tf_op jit(solution)/shard_map/ppermute | solution.py:208
  162.2 27.7 %copy-start.4 = (bf16[1344,512]{1,0:T(8,128)(2,1)}, bf16[1344,512]{1,0:T(8,128)(2,1)S(1)}, u32[]{:S(2)}) copy-start(bf16[1344,512]{1,0:T(8,128)(2,1)S(1)} %collective-permute-done.9.refs_4_) | copy-start | bytes 4128772
  162.2 2.7 %copy-start.5 = (bf16[1344,512]{1,0:T(8,128)(2,1)}, bf16[1344,512]{1,0:T(8,128)(2,1)S(1)}, u32[]{:S(2)}) copy-start(bf16[1344,512]{1,0:T(8,128)(2,1)S(1)} %collective-permute-done.8.refs_5_) | copy-start | bytes 4128772
  162.3 27.5 %collective-permute-start.10 = (bf16[672,512]{1,0:T(8,128)(2,1)S(1)}, bf16[672,512]{1,0:T(8,128)(2,1)S(1)}, u32[]{:S(2)}, u32[]{:S(2)}) collective-permute-start(bf16[672,512]{1,0:T(8,128)(2,1)S(1)} %slice.6), channel_id=1, source_target_pairs={{0,1},{1,0},{2,3},{3,2},{4,5},{5,4},{6,7},{7,6},{8,9},{9,8},{10,11... | collective-permute-start | bytes 2064392 | tf_op jit(solution)/shard_map/ppermute | solution.py:208
  163.3 26.6 %collective-permute-start.11 = (bf16[672,512]{1,0:T(8,128)(2,1)S(1)}, bf16[672,512]{1,0:T(8,128)(2,1)S(1)}, u32[]{:S(2)}, u32[]{:S(2)}) collective-permute-start(bf16[672,512]{1,0:T(8,128)(2,1)S(1)} %slice.7), channel_id=1, source_target_pairs={{0,2},{1,3},{2,0},{3,1},{4,6},{5,7},{6,4},{7,5},{8,10},{9,11},{10,... | collective-permute-start | bytes 2064392 | tf_op jit(solution)/shard_map/ppermute | solution.py:208
  189.9 0.8 copy-start.11
  190.7 0.9 copy-start.12

commit v2 on v0

--- a/solution.py
+++ b/solution.py
@@ -1,9 +1,16 @@
+import functools
+
 import jax
 import jax.numpy as jnp
 from jax import lax
+from jax.experimental import pallas as pl
+from jax.experimental.pallas import tpu as pltpu
 from jax.sharding import PartitionSpec as P
 
 STATES = 21
+LANE = 128
+LOCAL_VMEM = 36 * 2**20
+SPARE_VMEM = 10 * 2**20
 
 
 def from_behind(value, axis, steps):
@@ -20,7 +27,7 @@
     return jnp.stack(received, axis=0)
 
 
-def body(scores, counts):
+def plain_body(scores, counts):
     seq_rows = scores.shape[0]
     block_pos = scores.shape[1] // STATES
     raw = scores.astype(jnp.float32).reshape(seq_rows, block_pos, STATES)
@@ -39,11 +46,325 @@
     seq_index = lax.axis_index("seq")
     stripe_here = lax.dynamic_slice_in_dim(gathered, seq_index * stripe_width, stripe_width, 1)
     partners = partner_stripes(stripe_here)
-    covariance = jnp.einsum("kmr,mc->krc", partners, gathered, preferred_element_type=jnp.float32)
-    return covariance
+    return jnp.einsum("kmr,mc->krc", partners, gathered, preferred_element_type=jnp.float32)
+
+
+def payload_kernel(scores_ref, counts_ref, out_ref):
+    parts, rows, width = out_ref.shape
+    stripe = scores_ref.shape[1] // parts
+    counts = jnp.broadcast_to(counts_ref[...].astype(jnp.float32), (rows, rows)).T
+    tail = counts[:, : width - stripe].astype(jnp.bfloat16)
+    for j in range(parts):
+        out_ref[j, :, :stripe] = scores_ref[:, j * stripe : (j + 1) * stripe]
+        out_ref[j, :, stripe:] = tail
+
+
+def payload(scores, counts, parts):
+    rows, columns = scores.shape
+    stripe = columns // parts
+    vmem = pl.BlockSpec(memory_space=pltpu.VMEM)
+    return pl.pallas_call(
+        payload_kernel,
+        out_shape=jax.ShapeDtypeStruct((parts, rows, stripe + LANE // 2), jnp.bfloat16),
+        in_specs=[vmem, vmem],
+        out_specs=vmem,
+        compiler_params=pltpu.CompilerParams(vmem_limit_bytes=LOCAL_VMEM),
+        name="payload",
+    )(scores, counts.reshape(1, rows))
+
+
+def center_kernel(raw_ref, out_ref):
+    width = out_ref.shape[0]
+    pos = width // STATES
+    raw = raw_ref[:, :width]
+    counts = raw_ref[:, width:].astype(jnp.float32)[:, :1]
+
+    def members(copies):
+        shape = (copies * pos, width)
+        row = lax.broadcasted_iota(jnp.int32, shape, 0)
+        for _ in range(copies - 1):
+            row = jnp.where(row >= pos, row - pos, row)
+        first = STATES * row
+        here = lax.broadcasted_iota(jnp.int32, shape, 1)
+        return ((here >= first) & (here < first + STATES)).astype(jnp.bfloat16)
+
+    sums = lax.dot_general(
+        raw, members(1), (((1,), (1,)), ((), ())), preferred_element_type=jnp.float32
+    )
+    high = sums.astype(jnp.bfloat16)
+    rest = sums - high.astype(jnp.float32)
+    mid = rest.astype(jnp.bfloat16)
+    low = (rest - mid.astype(jnp.float32)).astype(jnp.bfloat16)
+    terms = jnp.concatenate([high, mid, low], axis=1)
+    spread = jnp.dot(terms, members(3), preferred_element_type=jnp.float32)
+    profile = raw.astype(jnp.float32) / spread
+    weight = 1.0 / counts
+    total = jnp.sum(weight, axis=0, keepdims=True)
+    freq = jnp.sum(weight * profile, axis=0, keepdims=True) / total
+    scaled = jnp.sqrt(weight * STATES / total)
+    centered = (scaled * (profile - freq)).astype(jnp.bfloat16)
+    out_ref[...] = centered.T
+
+
+def center(raw, stripe):
+    seqs = raw.shape[0]
+    vmem = pl.BlockSpec(memory_space=pltpu.VMEM)
+    return pl.pallas_call(
+        center_kernel,
+        out_shape=jax.ShapeDtypeStruct((stripe, seqs), jnp.bfloat16),
+        in_specs=[vmem],
+        out_specs=vmem,
+        compiler_params=pltpu.CompilerParams(vmem_limit_bytes=LOCAL_VMEM),
+        name="center",
+    )(raw)
+
+
+FIRST, SECOND, PAIR = "first", "second", "pair"
+
+
+def width_of(form, stripe):
+    whole = stripe // LANE * LANE
+    return {FIRST: whole, SECOND: 2 * stripe - whole, PAIR: 2 * stripe}[form]
+
+
+def fill_right(form, right, mine, other, x):
+    stripe = sum(ref.shape[0] for ref in mine)
+    width = right.shape[0]
+    whole = stripe // LANE * LANE
+    cut = stripe - whole
+
+    def rows(ref, start, size):
+        return ref[pl.ds(pl.multiple_of(start, 16), size), :]
+
+    def put(refs, row):
+        for ref in refs:
+            right[pl.ds(pl.multiple_of(row, 16), ref.shape[0]), :] = ref[...]
+            row = row + ref.shape[0]
+
+    if form == PAIR:
+        put(mine, x * stripe)
+        put(other, (1 - x) * stripe)
+        return 0
+    if form == SECOND:
+        put(other, (1 - x) * cut)
+
+        @pl.when(x == 0)
+        def _():
+            last = mine[-1]
+            right[:cut, :] = last[last.shape[0] - cut :, :]
+
+        @pl.when(x != 0)
+        def _():
+            right[stripe:, :] = mine[0][:cut, :]
+
+        return (1 - x) * ((2 * stripe - width) // LANE)
+
+    @pl.when(x == 0)
+    def _():
+        row = 0
+        for ref in mine:
+            size = min(ref.shape[0], width - row)
+            right[row : row + size, :] = ref[:size, :]
+            row += size
+
+    @pl.when(x != 0)
+    def _():
+        row, skip = 0, cut
+        for ref in mine:
+            size = ref.shape[0] - skip
+            right[row : row + size, :] = ref[skip:, :]
+            row, skip = row + size, 0
+
+    return x * ((2 * stripe - width) // LANE)
+
+
+def tiles_kernel(jobs, joining, aliased, slots, *refs):
+    if joining:
+        parts, refs = refs[:joining], refs[joining:]
+    else:
+        left, refs = refs[0], refs[1:]
+    pieces = []
+    for _, _, mine, other, _ in jobs:
+        pieces.append((refs[:mine], refs[mine : mine + other]))
+        refs = refs[mine + other :]
+    if aliased:
+        refs = refs[1:]
+    out, refs = refs[0], refs[1:]
+    if joining:
+        left, refs = refs[0], refs[1:]
+    rights, (out_buf, out_sem) = refs[:-2], refs[-2:]
+    seq, core = lax.axis_index("seq"), lax.rem(lax.axis_index("blk"), 2)
+    x, z = lax.rem(seq, 2), seq // 2
+    tall = out_buf.shape[1]
+    stripe = out.shape[1]
+    per = stripe // tall
+    if joining:
+        for j in range(joining):
+            left[j * stripe : (j + 1) * stripe, :] = parts[j][...]
+
+    def store(job, tile, step):
+        which = step // per
+        round_ = jnp.where(
+            which == 0, 0, jnp.where(which == 1, 3 - 2 * core, jnp.where(which == 2, 2, 1 + 2 * core))
+        )
+        width = rights[job].shape[0]
+        slot = lax.rem(step, slots)
+        row = pl.multiple_of(lax.rem(step, per) * tall, 16)
+        return pltpu.make_async_copy(
+            out_buf.at[slot, :, pl.ds(0, width)],
+            out.at[round_, pl.ds(row, tall), pl.ds(pl.multiple_of(tile * LANE, LANE), width)],
+            out_sem.at[slot],
+        )
+
+    before = None
+    for job, (form, flipped, _, _, (low, high)) in enumerate(jobs):
+        low, high = low * per, high * per
+        right = rights[job]
+        tile = (z ^ flipped) * (2 * stripe // LANE) + fill_right(form, right, *pieces[job], x)
+        here = functools.partial(store, job, tile)
+
+        def body(step, _, here=here, before=before, right=right, low=low):
+            if before is not None:
+
+                @pl.when(step < low + slots)
+                def _():
+                    before(step).wait()
+
+            @pl.when(step >= low + slots)
+            def _():
+                here(step).wait()
+
+            out_buf[lax.rem(step, slots), :, : right.shape[0]] = lax.dot_general(
+                left[pl.ds(pl.multiple_of(step * tall, 16), tall), :],
+                right[...],
+                (((1,), (1,)), ((), ())),
+                preferred_element_type=jnp.float32,
+            )
+            here(step).start()
+            return 0
+
+        lax.fori_loop(low, high, body, 0)
+        before = here
+    for slot in range(slots):
+        before(jnp.int32(slot)).wait()
+
+
+def tiles(out, out_shape, left, jobs, slots=4):
+    joining = len(left) if isinstance(left, list) else 0
+    stripe = out_shape[1]
+    depth = (left[0] if joining else left).shape[1]
+    tall = stripe // 4
+    widths = [width_of(form, stripe) for form, *_ in jobs]
+    vmem = pl.BlockSpec(memory_space=pltpu.VMEM)
+    anywhere = pl.BlockSpec(memory_space=pl.ANY)
+    operands = list(left) if joining else [left]
+    for _, _, mine, other, _ in jobs:
+        operands += [*mine, *other]
+    specs = [vmem] * len(operands)
+    aliases = {}
+    if out is not None:
+        aliases = {len(operands): 0}
+        operands.append(out)
+        specs.append(anywhere)
+    shapes, out_specs = [jax.ShapeDtypeStruct(out_shape, jnp.float32)], [anywhere]
+    if joining:
+        shapes.append(jax.ShapeDtypeStruct((joining * stripe, depth), jnp.bfloat16))
+        out_specs.append(vmem)
+    forms = [(form, pair, len(mine), len(other), part) for form, pair, mine, other, part in jobs]
+    scratch = sum(widths) * depth * 2 + slots * tall * max(widths) * 4
+    columns = sum(width * (part[1] - part[0]) for width, (*_, part) in zip(widths, jobs))
+    result = pl.pallas_call(
+        functools.partial(tiles_kernel, forms, joining, out is not None, slots),
+        out_shape=shapes,
+        in_specs=specs,
+        out_specs=out_specs,
+        scratch_shapes=[pltpu.VMEM((width, depth), jnp.bfloat16) for width in widths]
+        + [
+            pltpu.VMEM((slots, tall, max(widths)), jnp.float32),
+            pltpu.SemaphoreType.DMA((slots,)),
+        ],
+        input_output_aliases=aliases,
+        compiler_params=pltpu.CompilerParams(vmem_limit_bytes=scratch + SPARE_VMEM),
+        cost_estimate=pl.CostEstimate(
+            flops=2 * stripe * columns * depth,
+            bytes_accessed=4 * stripe * columns,
+            transcendentals=0,
+        ),
+        name="tiles",
+    )(*operands)
+    return result if joining else result[0]
+
+
+def flip(value, axis, bits):
+    count = lax.axis_size(axis)
+    return lax.ppermute(value, axis, [(source, source ^ bits) for source in range(count)])
+
+
+def wait_all(*values):
+    return lax.optimization_barrier(values)
+
+
+def fast_body(scores, counts):
+    blocks, parts = lax.axis_size("blk"), lax.axis_size("seq")
+    stripe = scores.shape[1] // parts
+    out_shape = (blocks, stripe, scores.shape[1])
+    raw = lax.all_to_all(payload(scores, counts, parts), "seq", 0, 0, tiled=True)
+    own = center(raw.reshape(-1, raw.shape[-1]), stripe)
+
+    z = lax.axis_index("seq") // 2
+    middle = (z == 1) | (z == 2)
+    z1 = flip(own, "seq", 2)
+    x_own = flip(own, "seq", 1)
+    z3_middle = lax.ppermute(own, "seq", [(2, 4), (4, 2), (3, 5), (5, 3)])
+    y_own = flip(own, "blk", 2)
+    core_own = flip(own, "blk", 1)
+    z3_outer = lax.ppermute(own, "seq", [(0, 6), (6, 0), (1, 7), (7, 1)])
+    out, _ = tiles(None, out_shape, [own, core_own], [(FIRST, 0, [own], [], (0, 2))])
+    own, x_own, z1, z3_middle, y_own, core_own, out = wait_all(
+        own, x_own, z1, z3_middle, y_own, core_own, out
+    )
+    x_z1 = flip(z1, "seq", 1)
+    core_y = flip(y_own, "blk", 1)
+    every = (0, 4)
+    out, left = tiles(
+        out,
+        out_shape,
+        [own, core_own, y_own, core_y],
+        [
+            (SECOND, 0, [own], [x_own], every),
+            (FIRST, 0, [own], [], (2, 4)),
+            (FIRST, 1, [z1], [], every),
+        ],
+    )
+    out, x_z1, z3_outer = wait_all(out, x_z1, z3_outer)
+    half = stripe // 2
+    z3 = [
+        jnp.where(middle, z3_middle[rows], z3_outer[rows])
+        for rows in (slice(0, half), slice(half, stripe))
+    ]
+    x_z3_low = flip(z3[1], "seq", 1)
+    z2_top = flip(z3[0], "seq", 2)
+    x_z3 = [flip(z3[0], "seq", 1), x_z3_low]
+    z2 = [z2_top, flip(z3[1], "seq", 2)]
+    out = tiles(out, out_shape, left, [(SECOND, 1, [z1], [x_z1], every), (FIRST, 3, z3, [], every)])
+    out, z2[0], x_z3[1] = wait_all(out, z2[0], x_z3[1])
+    x_z2 = [flip(z2[0], "seq", 1), flip(x_z3[1], "seq", 2)]
+    out = tiles(out, out_shape, left, [(SECOND, 3, z3, x_z3, every), (FIRST, 2, z2, [], every)])
+    return tiles(out, out_shape, left, [(SECOND, 2, z2, x_z2, every)])
 
 
 def solution(mesh):
+    def body(scores, counts):
+        stripe_width = scores.shape[1] // mesh.shape["seq"]
+        fits = (
+            mesh.shape["blk"] == 4
+            and mesh.shape["seq"] == 8
+            and stripe_width % 64 == 0
+            and stripe_width % STATES == 0
+            and stripe_width % 64 == 0
+        )
+        return (fast_body if fits else plain_body)(scores, counts)
+
     return jax.shard_map(
         body,
         mesh=mesh,

time: 396 us -> 192 us (0.48)
  waiting for transfers between devices: 215 us -> 26.8 us
  Pallas kernels: 0 us -> 101 us
  matrix products: 84 us -> 0 us
  local copies, waits for them, and re-layouts: 26.9 us -> 6.31 us
  starting transfers between devices: 1.77 us -> 15.5 us
  other arithmetic: 13.5 us -> 0.14 us
  between operations: 13.4 us -> 0.14 us
    all_gather x1 -> x0, waiting for transfers between devices: 155 us -> none  [body(): gathered = lax.all_gather(centered, 'seq', axis=0, tiled=True)]
    pallas_call x0 -> x7, Pallas kernels: none -> 101 us  [the longest x5 99.2 us: tiles(): pl.pallas_call(functools.partial(tiles_kernel, forms, joining, out is not...]
    dot_general x1 -> x0, matrix products: 84 us -> none  [body(): jnp.einsum('kmr,mc->krc', partners, gathered, preferred_element_type=jnp....]
    all_to_all x0 -> x1, blocking collectives: none -> 41.6 us  [fast_body(): lax.all_to_all(payload(scores, counts, parts), 'seq', 0, 0, tiled=True)]
    psum x1 -> x0, blocking collectives: 40.3 us -> none  [body(): lax.psum((jnp.sum(weight), jnp.sum(weight[:, None] * profile, axis=0)), '...]
    ppermute x3 -> x14, waiting for transfers between devices: 60.3 us -> 26.8 us  [the longest x12 26.8 us: flip(): lax.ppermute(value, axis, [(source, source ^ bits) for source in range(co...]
    ppermute x3 -> x14, starting transfers between devices: 1.77 us -> 15.5 us  [the longest x12 11.6 us: flip(): lax.ppermute(value, axis, [(source, source ^ bits) for source in range(co...]
    div x2 -> x0, local copies, waits for them, and re-layouts: 10.8 us -> none  [body(): profile = raw / jnp.sum(raw, axis=2, keepdims=True)]
  transfers between devices with their start and end apart: 4 -> 14, of which waited for: 4 -> 3; matrix products, arithmetic and copies ran while one was open for 0% -> 0% of each run, Pallas kernels for 0% -> 45%
where the time goes in v2:
time: 192 us
  Pallas kernels  101 us (53%)
  blocking collectives  41.6 us (22%)
  waiting for transfers between devices  26.8 us (14%)
  starting transfers between devices  15.5 us (8%)
  local copies, waits for them, and re-layouts  6.31 us (3%)
    pallas_call x5, Pallas kernels, tiles(): pl.pallas_call(functools.partial(tiles_kernel, forms, joining, out is not...  99.2 us
    all_to_all x1, blocking collectives, fast_body(): lax.all_to_all(payload(scores, counts, parts), 'seq', 0, 0, tiled=True)  41.6 us
    ppermute x12, waiting for transfers between devices, flip(): lax.ppermute(value, axis, [(source, source ^ bits) for source in range(co...  26.8 us
    ppermute x12, starting transfers between devices, flip(): lax.ppermute(value, axis, [(source, source ^ bits) for source in range(co...  11.6 us
    unnamed x16, local copies, waits for them, and re-layouts  6.31 us
  transfers between devices with their start and end apart: 14, of which 3 were waited for; matrix products, arithmetic and copies ran while one was open for 0% of the time, Pallas kernels for 45%

profile of v2, /device:TPU:0, one launch (start us, length us, event | category | flops | bytes accessed | tf_op | source)
XLA Modules:
  0.0 192.0 jit_solution(1216447631213941686)
XLA Ops:
  0.0 1.3 copy-done.4
  1.3 0.7 copy-done.5
  2.0 0.3 payload.1
  2.3 41.6 %all_to_all.5 = bf16[8,64,1408]{2,1,0:T(8,128)(2,1)S(1)} all-to-all(bf16[8,64,1408]{2,1,0:T(8,128)(2,1)S(1)} %payload.1), channel_id=1, replica_groups=mesh['blk'=4,'seq'=8] {'seq'}, dimensions={0} | all-to-all | bytes 2883584 | tf_op jit(solution)/shard_map/all_to_all | solution.py:311
  43.9 1.9 center.1.refs_0_.refs_2_.refs_4_.refs_6_
  45.8 0.1 collective-permute-start.4
  45.9 1.2 collective-permute-start
  47.1 0.2 collective-permute-start.1
  47.3 0.7 collective-permute-start.2
  48.0 1.6 collective-permute-start.3
  49.6 0.0 collective-permute-done.4.refs_1_
  49.6 8.2 %tiles.5 = (f32[4,1344,10752]{2,1,0:T(8,128)}, bf16[2688,512]{1,0:T(8,128)(2,1)}) custom-call(bf16[1344,512]{1,0:T(8,128)(2,1)S(1)} %center.1.refs_0_.refs_2_.refs_4_.refs_6_, bf16[1344,512]{1,0:T(8,128)(2,1)S(1)} %collective-permute-done.4.refs_1_, bf16[1344,512]{1,0:T(8,128)(2,1)S(1)} %center.1.refs_0_.refs_2_.refs_4_.refs_6_), custom_call_target="tpu_custom_call" | custom-call | flops 3523215360 | bytes 13762560 | tf_op jit(solution)/shard_map/tiles/pallas_call | solution.py:276
  57.9 20.6 %collective-permute-done.refs_5_ = bf16[1344,512]{1,0:T(8,128)(2,1)S(1)} collective-permute-done((bf16[1344,512]{1,0:T(8,128)(2,1)S(1)}, bf16[1344,512]{1,0:T(8,128)(2,1)S(1)}, u32[]{:S(2)}, u32[]{:S(2)}) %collective-permute-start) | collective-permute-done | bytes 1376288 | tf_op jit(solution)/shard_map/ppermute | solution.py:300
  78.5 1.1 copy-done.2
  79.7 0.6 collective-permute-done.3.refs_2_
  80.2 0.5 copy-done.6
  80.8 3.2 %collective-permute-start.7 = (bf16[1344,512]{1,0:T(8,128)(2,1)S(1)}, bf16[1344,512]{1,0:T(8,128)(2,1)S(1)}, u32[]{:S(2)}, u32[]{:S(2)}) collective-permute-start(bf16[1344,512]{1,0:T(8,128)(2,1)S(1)} %center.1.refs_0_.refs_2_.refs_4_.refs_6_), channel_id=1, source_target_pairs={{0,6},{6,0},{1,7},{7,1},{8,14},{14,8},{9,15},{15,9},{16,22},{22,16... | collective-permute-start | bytes 4128776 | tf_op jit(solution)/shard_map/ppermute | solution.py:321
  84.0 1.2 collective-permute-start.6
  85.2 1.3 copy-done.1
  86.6 1.3 copy-done.3
  87.9 30.9 %tiles.6 = (f32[4,1344,10752]{2,1,0:T(8,128)}, bf16[5376,512]{1,0:T(8,128)(2,1)S(1)}) custom-call(bf16[1344,512]{1,0:T(8,128)(2,1)S(1)} %center.1.refs_0_.refs_2_.refs_4_.refs_6_, bf16[1344,512]{1,0:T(8,128)(2,1)S(1)} %copy-done.1, bf16[1344,512]{1,0:T(8,128)(2,1)} %collective-permute-done.3.refs_2_, ...), custom_call_target="tpu_custom_call", output_to_operand_aliasing={{0}: (8, {})} | custom-call | flops 18320719872 | bytes 71565312 | tf_op jit(solution)/shard_map/tiles/pallas_call | solution.py:276
  118.9 0.1 slice_select_fusion
  119.0 0.9 collective-permute-start.9
  120.0 2.3 %collective-permute-start.10 = (bf16[672,512]{1,0:T(8,128)(2,1)S(1)}, bf16[672,512]{1,0:T(8,128)(2,1)S(1)}, u32[]{:S(2)}, u32[]{:S(2)}) collective-permute-start(bf16[672,512]{1,0:T(8,128)(2,1)S(1)} %get-tuple-element.37.refs_4_.refs_2_), channel_id=1, source_target_pairs={{0,2},{1,3},{2,0},{3,1},{4,6},{5,7},{6,4},{7,5},{8,10},{9,11},{10,... | collective-permute-start | bytes 2064392 | tf_op jit(solution)/shard_map/ppermute | solution.py:300
  122.3 0.0 collective-permute-start.8
  122.3 1.2 collective-permute-start.13
  123.5 23.4 %tiles.7.refs_7_ = f32[4,1344,10752]{2,1,0:T(8,128)} custom-call(bf16[5376,512]{1,0:T(8,128)(2,1)S(1)} %get-tuple-element.28.refs_0_, bf16[1344,512]{1,0:T(8,128)(2,1)S(1)} %collective-permute-done.1.refs_7_.refs_1_, bf16[1344,512]{1,0:T(8,128)(2,1)S(1)} %collective-permute-done.6.refs_2_, ...), custom_call_target="tpu_custom_call", output_to_operand_aliasing={{}: (5, {})} | custom-call | flops 14797504512 | bytes 57802752 | tf_op jit(solution)/shard_map/tiles/pallas_call | solution.py:276
  147.0 5.5 %collective-permute-done.8.refs_5_.refs_1_ = bf16[672,512]{1,0:T(8,128)(2,1)S(1)} collective-permute-done((bf16[672,512]{1,0:T(8,128)(2,1)S(1)}, bf16[672,512]{1,0:T(8,128)(2,1)S(1)}, u32[]{:S(2)}, u32[]{:S(2)}) %collective-permute-start.8) | collective-permute-done | bytes 688160 | tf_op jit(solution)/shard_map/ppermute | solution.py:300
  152.5 1.1 collective-permute-start.11
  153.6 1.7 collective-permute-start.12
  155.4 23.4 %tiles.8.refs_5_ = f32[4,1344,10752]{2,1,0:T(8,128)} custom-call(bf16[5376,512]{1,0:T(8,128)(2,1)S(1)} %get-tuple-element.28.refs_0_, bf16[672,512]{1,0:T(8,128)(2,1)S(1)} %get-tuple-element.38.refs_3_.refs_1_, bf16[672,512]{1,0:T(8,128)(2,1)S(1)} %get-tuple-element.37.refs_4_.refs_2_, ...), custom_call_target="tpu_custom_call", output_to_operand_aliasing={{}: (7, {})} | custom-call | flops 14797504512 | bytes 57802752 | tf_op jit(solution)/shard_map/tiles/pallas_call | solution.py:276
  178.8 13.1 %tiles.9 = f32[4,1344,10752]{2,1,0:T(8,128)} custom-call(bf16[5376,512]{1,0:T(8,128)(2,1)S(1)} %get-tuple-element.28.refs_0_, bf16[672,512]{1,0:T(8,128)(2,1)S(1)} %collective-permute-done.8.refs_5_.refs_1_, bf16[672,512]{1,0:T(8,128)(2,1)S(1)} %collective-permute-done.10.refs_6_.refs_2_, ...), custom_call_target="tpu_custom_call", output_to_operand_aliasing={{}: (5, {})} | custom-call | flops 7751073792 | bytes 30277632 | tf_op jit(solution)/shard_map/tiles/pallas_call | solution.py:276
  (21 shorter events, 0.0 us)
Async XLA Ops:
  0.0 1.3 copy-start.4
  1.3 0.7 copy-start.5
  45.8 3.8 %collective-permute-start.4 = (bf16[1344,512]{1,0:T(8,128)(2,1)S(1)}, bf16[1344,512]{1,0:T(8,128)(2,1)S(1)}, u32[]{:S(2)}, u32[]{:S(2)}) collective-permute-start(bf16[1344,512]{1,0:T(8,128)(2,1)S(1)} %center.1.refs_0_.refs_2_.refs_4_.refs_6_), channel_id=1, source_target_pairs={{0,8},{8,0},{16,24},{24,16},{1,9},{9,1},{17,25},{25,17},{2,10},{10... | collective-permute-start | bytes 4128776 | tf_op jit(solution)/shard_map/ppermute | solution.py:300
  45.9 32.6 %collective-permute-start = (bf16[1344,512]{1,0:T(8,128)(2,1)S(1)}, bf16[1344,512]{1,0:T(8,128)(2,1)S(1)}, u32[]{:S(2)}, u32[]{:S(2)}) collective-permute-start(bf16[1344,512]{1,0:T(8,128)(2,1)S(1)} %center.1.refs_0_.refs_2_.refs_4_.refs_6_), channel_id=1, source_target_pairs={{0,1},{1,0},{2,3},{3,2},{4,5},{5,4},{6,7},{7,6},{8,9},{9,8},{10,11... | collective-permute-start | bytes 4128776 | tf_op jit(solution)/shard_map/ppermute | solution.py:300
  47.1 32.6 %collective-permute-start.1 = (bf16[1344,512]{1,0:T(8,128)(2,1)S(1)}, bf16[1344,512]{1,0:T(8,128)(2,1)S(1)}, u32[]{:S(2)}, u32[]{:S(2)}) collective-permute-start(bf16[1344,512]{1,0:T(8,128)(2,1)S(1)} %center.1.refs_0_.refs_2_.refs_4_.refs_6_), channel_id=1, source_target_pairs={{0,2},{1,3},{2,0},{3,1},{4,6},{5,7},{6,4},{7,5},{8,10},{9,11},{10,... | collective-permute-start | bytes 4128776 | tf_op jit(solution)/shard_map/ppermute | solution.py:300
  47.3 32.4 %collective-permute-start.2 = (bf16[1344,512]{1,0:T(8,128)(2,1)S(1)}, bf16[1344,512]{1,0:T(8,128)(2,1)S(1)}, u32[]{:S(2)}, u32[]{:S(2)}) collective-permute-start(bf16[1344,512]{1,0:T(8,128)(2,1)S(1)} %center.1.refs_0_.refs_2_.refs_4_.refs_6_), channel_id=1, source_target_pairs={{2,4},{4,2},{3,5},{5,3},{10,12},{12,10},{11,13},{13,11},{18,20},{2... | collective-permute-start | bytes 4128776 | tf_op jit(solution)/shard_map/ppermute | solution.py:318
  48.0 32.2 %collective-permute-start.3 = (bf16[1344,512]{1,0:T(8,128)(2,1)S(1)}, bf16[1344,512]{1,0:T(8,128)(2,1)}, u32[]{:S(2)}, u32[]{:S(2)}) collective-permute-start(bf16[1344,512]{1,0:T(8,128)(2,1)S(1)} %center.1.refs_0_.refs_2_.refs_4_.refs_6_), channel_id=1, source_target_pairs={{0,16},{8,24},{16,0},{24,8},{1,17},{9,25},{17,1},{25,9},{2,18},{10... | collective-permute-start | bytes 4128776 | tf_op jit(solution)/shard_map/ppermute | solution.py:300
  49.6 8.2 %copy-start = (bf16[1344,512]{1,0:T(8,128)(2,1)}, bf16[1344,512]{1,0:T(8,128)(2,1)S(1)}, u32[]{:S(2)}) copy-start(bf16[1344,512]{1,0:T(8,128)(2,1)S(1)} %collective-permute-done.4.refs_1_) | copy-start | bytes 4128772
  78.5 1.1 copy-start.2
  79.7 1.1 copy-start.6
  80.7 4.5 %collective-permute-start.5 = (bf16[1344,512]{1,0:T(8,128)(2,1)}, bf16[1344,512]{1,0:T(8,128)(2,1)}, u32[]{:S(2)}, u32[]{:S(2)}) collective-permute-start(bf16[1344,512]{1,0:T(8,128)(2,1)} %collective-permute-done.3.refs_2_), channel_id=1, source_target_pairs={{0,8},{8,0},{16,24},{24,16},{1,9},{9,1},{17,25},{25,17},{2,10},{10... | collective-permute-start | bytes 4128776 | tf_op jit(solution)/shard_map/ppermute | solution.py:300
  80.8 38.1 %collective-permute-start.7 = (bf16[1344,512]{1,0:T(8,128)(2,1)S(1)}, bf16[1344,512]{1,0:T(8,128)(2,1)S(1)}, u32[]{:S(2)}, u32[]{:S(2)}) collective-permute-start(bf16[1344,512]{1,0:T(8,128)(2,1)S(1)} %center.1.refs_0_.refs_2_.refs_4_.refs_6_), channel_id=1, source_target_pairs={{0,6},{6,0},{1,7},{7,1},{8,14},{14,8},{9,15},{15,9},{16,22},{22,16... | collective-permute-start | bytes 4128776 | tf_op jit(solution)/shard_map/ppermute | solution.py:321
  84.0 34.9 %collective-permute-start.6 = (bf16[1344,512]{1,0:T(8,128)(2,1)S(1)}, bf16[1344,512]{1,0:T(8,128)(2,1)S(1)}, u32[]{:S(2)}, u32[]{:S(2)}) collective-permute-start(bf16[1344,512]{1,0:T(8,128)(2,1)S(1)} %collective-permute-done.1.refs_7_.refs_1_), channel_id=1, source_target_pairs={{0,1},{1,0},{2,3},{3,2},{4,5},{5,4},{6,7},{7,6},{8,9},{9,8},{10,11... | collective-permute-start | bytes 4128776 | tf_op jit(solution)/shard_map/ppermute | solution.py:300
  85.2 1.3 copy-start.1
  86.6 1.3 copy-start.3
  87.9 31.0 %copy-start.7 = (bf16[1344,512]{1,0:T(8,128)(2,1)S(1)}, bf16[1344,512]{1,0:T(8,128)(2,1)}, u32[]{:S(2)}) copy-start(bf16[1344,512]{1,0:T(8,128)(2,1)} %copy-done.6) | copy-start | bytes 4128772
  119.0 33.5 %collective-permute-start.9 = (bf16[672,512]{1,0:T(8,128)(2,1)S(1)}, bf16[672,512]{1,0:T(8,128)(2,1)S(1)}, u32[]{:S(2)}, u32[]{:S(2)}) collective-permute-start(bf16[672,512]{1,0:T(8,128)(2,1)S(1)} %get-tuple-element.37.refs_4_.refs_2_), channel_id=1, source_target_pairs={{0,1},{1,0},{2,3},{3,2},{4,5},{5,4},{6,7},{7,6},{8,9},{9,8},{10,11... | collective-permute-start | bytes 2064392 | tf_op jit(solution)/shard_map/ppermute | solution.py:300
  120.0 35.4 %collective-permute-start.10 = (bf16[672,512]{1,0:T(8,128)(2,1)S(1)}, bf16[672,512]{1,0:T(8,128)(2,1)S(1)}, u32[]{:S(2)}, u32[]{:S(2)}) collective-permute-start(bf16[672,512]{1,0:T(8,128)(2,1)S(1)} %get-tuple-element.37.refs_4_.refs_2_), channel_id=1, source_target_pairs={{0,2},{1,3},{2,0},{3,1},{4,6},{5,7},{6,4},{7,5},{8,10},{9,11},{10,... | collective-permute-start | bytes 2064392 | tf_op jit(solution)/shard_map/ppermute | solution.py:300
  122.3 30.2 %collective-permute-start.8 = (bf16[672,512]{1,0:T(8,128)(2,1)S(1)}, bf16[672,512]{1,0:T(8,128)(2,1)S(1)}, u32[]{:S(2)}, u32[]{:S(2)}) collective-permute-start(bf16[672,512]{1,0:T(8,128)(2,1)S(1)} %get-tuple-element.38.refs_3_.refs_1_), channel_id=1, source_target_pairs={{0,2},{1,3},{2,0},{3,1},{4,6},{5,7},{6,4},{7,5},{8,10},{9,11},{10,... | collective-permute-start | bytes 2064392 | tf_op jit(solution)/shard_map/ppermute | solution.py:300
  122.3 33.0 %collective-permute-start.13 = (bf16[672,512]{1,0:T(8,128)(2,1)S(1)}, bf16[672,512]{1,0:T(8,128)(2,1)S(1)}, u32[]{:S(2)}, u32[]{:S(2)}) collective-permute-start(bf16[672,512]{1,0:T(8,128)(2,1)S(1)} %get-tuple-element.38.refs_3_.refs_1_), channel_id=1, source_target_pairs={{0,1},{1,0},{2,3},{3,2},{4,5},{5,4},{6,7},{7,6},{8,9},{9,8},{10,11... | collective-permute-start | bytes 2064392 | tf_op jit(solution)/shard_map/ppermute | solution.py:300
  152.5 26.3 %collective-permute-start.11 = (bf16[672,512]{1,0:T(8,128)(2,1)S(1)}, bf16[672,512]{1,0:T(8,128)(2,1)S(1)}, u32[]{:S(2)}, u32[]{:S(2)}) collective-permute-start(bf16[672,512]{1,0:T(8,128)(2,1)S(1)} %collective-permute-done.8.refs_5_.refs_1_), channel_id=1, source_target_pairs={{0,1},{1,0},{2,3},{3,2},{4,5},{5,4},{6,7},{7,6},{8,9},{9,8},{10,11... | collective-permute-start | bytes 2064392 | tf_op jit(solution)/shard_map/ppermute | solution.py:300
  153.6 25.2 %collective-permute-start.12 = (bf16[672,512]{1,0:T(8,128)(2,1)S(1)}, bf16[672,512]{1,0:T(8,128)(2,1)S(1)}, u32[]{:S(2)}, u32[]{:S(2)}) collective-permute-start(bf16[672,512]{1,0:T(8,128)(2,1)S(1)} %collective-permute-done.9.refs_4_), channel_id=1, source_target_pairs={{0,2},{1,3},{2,0},{3,1},{4,6},{5,7},{6,4},{7,5},{8,10},{9,11},{10,... | collective-permute-start | bytes 2064392 | tf_op jit(solution)/shard_map/ppermute | solution.py:300

commit v3 on v2

--- a/solution.py
+++ b/solution.py
@@ -49,32 +49,41 @@
     return jnp.einsum("kmr,mc->krc", partners, gathered, preferred_element_type=jnp.float32)
 
 
-def payload_kernel(scores_ref, counts_ref, out_ref):
-    parts, rows, width = out_ref.shape
+def payload_kernel(scores_ref, counts_ref, *refs):
+    out, cut = refs[:-1], refs[-1]
+    parts, rows, width = cut.shape
     stripe = scores_ref.shape[1] // parts
     counts = jnp.broadcast_to(counts_ref[...].astype(jnp.float32), (rows, rows)).T
     tail = counts[:, : width - stripe].astype(jnp.bfloat16)
     for j in range(parts):
-        out_ref[j, :, :stripe] = scores_ref[:, j * stripe : (j + 1) * stripe]
-        out_ref[j, :, stripe:] = tail
+        cut[j, :, :stripe] = scores_ref[:, j * stripe : (j + 1) * stripe]
+        cut[j, :, stripe:] = tail
+    for m in range(parts):
+        out[m][...] = cut[lax.axis_index("seq") ^ m]
 
 
 def payload(scores, counts, parts):
     rows, columns = scores.shape
-    stripe = columns // parts
+    width = columns // parts + LANE // 2
     vmem = pl.BlockSpec(memory_space=pltpu.VMEM)
     return pl.pallas_call(
         payload_kernel,
-        out_shape=jax.ShapeDtypeStruct((parts, rows, stripe + LANE // 2), jnp.bfloat16),
+        out_shape=[jax.ShapeDtypeStruct((rows, width), jnp.bfloat16)] * parts,
         in_specs=[vmem, vmem],
-        out_specs=vmem,
+        out_specs=[vmem] * parts,
+        scratch_shapes=[pltpu.VMEM((parts, rows, width), jnp.bfloat16)],
         compiler_params=pltpu.CompilerParams(vmem_limit_bytes=LOCAL_VMEM),
         name="payload",
     )(scores, counts.reshape(1, rows))
 
 
-def center_kernel(raw_ref, out_ref):
+def center_kernel(order, *refs):
+    pieces, out_ref, raw_ref = refs[:-2], refs[-2], refs[-1]
     width = out_ref.shape[0]
+    for bits, piece in zip(order, pieces):
+        rows = piece.shape[0]
+        first = pl.multiple_of((lax.axis_index("seq") ^ bits) * rows, 16)
+        raw_ref[pl.ds(first, rows), :] = piece[...]
     pos = width // STATES
     raw = raw_ref[:, :width]
     counts = raw_ref[:, width:].astype(jnp.float32)[:, :1]
@@ -106,17 +115,19 @@
     out_ref[...] = centered.T
 
 
-def center(raw, stripe):
-    seqs = raw.shape[0]
+def center(order, pieces, stripe):
+    rows, width = pieces[0].shape
+    seqs = rows * len(pieces)
     vmem = pl.BlockSpec(memory_space=pltpu.VMEM)
     return pl.pallas_call(
-        center_kernel,
+        functools.partial(center_kernel, order),
         out_shape=jax.ShapeDtypeStruct((stripe, seqs), jnp.bfloat16),
-        in_specs=[vmem],
+        in_specs=[vmem] * len(pieces),
         out_specs=vmem,
+        scratch_shapes=[pltpu.VMEM((seqs, width), jnp.bfloat16)],
         compiler_params=pltpu.CompilerParams(vmem_limit_bytes=LOCAL_VMEM),
         name="center",
-    )(raw)
+    )(*pieces)
 
 
 FIRST, SECOND, PAIR = "first", "second", "pair"
@@ -202,13 +213,13 @@
         for j in range(joining):
             left[j * stripe : (j + 1) * stripe, :] = parts[j][...]
 
-    def store(job, tile, step):
+    def store(job, tile, shift, step):
         which = step // per
         round_ = jnp.where(
             which == 0, 0, jnp.where(which == 1, 3 - 2 * core, jnp.where(which == 2, 2, 1 + 2 * core))
         )
         width = rights[job].shape[0]
-        slot = lax.rem(step, slots)
+        slot = lax.rem(step + shift, slots)
         row = pl.multiple_of(lax.rem(step, per) * tall, 16)
         return pltpu.make_async_copy(
             out_buf.at[slot, :, pl.ds(0, width)],
@@ -216,25 +227,26 @@
             out_sem.at[slot],
         )
 
-    before = None
+    before, shift = None, 0
     for job, (form, flipped, _, _, (low, high)) in enumerate(jobs):
         low, high = low * per, high * per
+        shift -= low
         right = rights[job]
         tile = (z ^ flipped) * (2 * stripe // LANE) + fill_right(form, right, *pieces[job], x)
-        here = functools.partial(store, job, tile)
-
-        def body(step, _, here=here, before=before, right=right, low=low):
+        here = functools.partial(store, job, tile, shift % slots)
+
+        def body(step, _, here=here, before=before, right=right, low=low, shift=shift % slots):
             if before is not None:
 
                 @pl.when(step < low + slots)
                 def _():
-                    before(step).wait()
+                    before(step - low).wait()
 
             @pl.when(step >= low + slots)
             def _():
                 here(step).wait()
 
-            out_buf[lax.rem(step, slots), :, : right.shape[0]] = lax.dot_general(
+            out_buf[lax.rem(step + shift, slots), :, : right.shape[0]] = lax.dot_general(
                 left[pl.ds(pl.multiple_of(step * tall, 16), tall), :],
                 right[...],
                 (((1,), (1,)), ((), ())),
@@ -244,16 +256,17 @@
             return 0
 
         lax.fori_loop(low, high, body, 0)
-        before = here
-    for slot in range(slots):
-        before(jnp.int32(slot)).wait()
-
-
-def tiles(out, out_shape, left, jobs, slots=4):
+        shift += high
+        before = functools.partial(store, job, tile, shift % slots)
+    for step in range(slots):
+        before(jnp.int32(step)).wait()
+
+
+def tiles(out, out_shape, left, jobs, slots=3):
     joining = len(left) if isinstance(left, list) else 0
     stripe = out_shape[1]
     depth = (left[0] if joining else left).shape[1]
-    tall = stripe // 4
+    tall = stripe // 2
     widths = [width_of(form, stripe) for form, *_ in jobs]
     vmem = pl.BlockSpec(memory_space=pltpu.VMEM)
     anywhere = pl.BlockSpec(memory_space=pl.ANY)
@@ -308,8 +321,13 @@
     blocks, parts = lax.axis_size("blk"), lax.axis_size("seq")
     stripe = scores.shape[1] // parts
     out_shape = (blocks, stripe, scores.shape[1])
-    raw = lax.all_to_all(payload(scores, counts, parts), "seq", 0, 0, tiled=True)
-    own = center(raw.reshape(-1, raw.shape[-1]), stripe)
+    pieces = payload(scores, counts, parts)
+    order = (6, 7, 4, 5, 2, 3, 1, 0)
+    own = center(
+        order,
+        [flip(pieces[bits], "seq", bits) if bits else pieces[0] for bits in order],
+        stripe,
+    )
 
     z = lax.axis_index("seq") // 2
     middle = (z == 1) | (z == 2)
@@ -320,9 +338,7 @@
     core_own = flip(own, "blk", 1)
     z3_outer = lax.ppermute(own, "seq", [(0, 6), (6, 0), (1, 7), (7, 1)])
     out, _ = tiles(None, out_shape, [own, core_own], [(FIRST, 0, [own], [], (0, 2))])
-    own, x_own, z1, z3_middle, y_own, core_own, out = wait_all(
-        own, x_own, z1, z3_middle, y_own, core_own, out
-    )
+    x_own, z1, z3_middle, y_own, out = wait_all(x_own, z1, z3_middle, y_own, out)
     x_z1 = flip(z1, "seq", 1)
     core_y = flip(y_own, "blk", 1)
     every = (0, 4)

time: 192 us -> 182 us (0.948)
  blocking collectives: 41.6 us -> 0 us
  starting transfers between devices: 15.5 us -> 43.5 us
  waiting for transfers between devices: 26.8 us -> 40.3 us
  Pallas kernels: 101 us -> 92 us
    all_to_all x1 -> x0, blocking collectives: 41.6 us -> none  [fast_body(): lax.all_to_all(payload(scores, counts, parts), 'seq', 0, 0, tiled=True)]
    ppermute x12 -> x19, starting transfers between devices: 11.6 us -> 38.1 us  [flip(): lax.ppermute(value, axis, [(source, source ^ bits) for source in range(co...]
    ppermute x12 -> x19, waiting for transfers between devices: 26.8 us -> 39.7 us  [flip(): lax.ppermute(value, axis, [(source, source ^ bits) for source in range(co...]
    pallas_call x5, Pallas kernels: 99.2 us -> 89.6 us  [tiles(): pl.pallas_call(functools.partial(tiles_kernel, forms, joining, out is not...]
  transfers between devices with their start and end apart: 14 -> 21, of which waited for: 3 -> 8; matrix products, arithmetic and copies ran while one was open for 0% -> 0% of each run, Pallas kernels for 45% -> 43%
where the time goes in v3:
time: 182 us
  Pallas kernels  92 us (51%)
  starting transfers between devices  43.5 us (24%)
  waiting for transfers between devices  40.3 us (22%)
  local copies, waits for them, and re-layouts  5.81 us (3%)
    pallas_call x5, Pallas kernels, tiles(): pl.pallas_call(functools.partial(tiles_kernel, forms, joining, out is not...  89.6 us
    ppermute x19, waiting for transfers between devices, flip(): lax.ppermute(value, axis, [(source, source ^ bits) for source in range(co...  39.7 us
    ppermute x19, starting transfers between devices, flip(): lax.ppermute(value, axis, [(source, source ^ bits) for source in range(co...  38.1 us
    unnamed x16, local copies, waits for them, and re-layouts  5.81 us
    ppermute x1, starting transfers between devices, fast_body(): z3_outer = lax.ppermute(own, 'seq', [(0, 6), (6, 0), (1, 7), (7, 1)])  4.64 us
  transfers between devices with their start and end apart: 21, of which 8 were waited for; matrix products, arithmetic and copies ran while one was open for 0% of the time, Pallas kernels for 43%

profile of v3, /device:TPU:0, one launch (start us, length us, event | category | flops | bytes accessed | tf_op | source)
XLA Modules:
  0.0 182.0 jit_solution(8137186021350290845)
XLA Ops:
  0.0 1.3 copy-done.4
  1.3 0.7 copy-done.5
  2.4 5.1 %collective-permute-start = (bf16[64,1408]{1,0:T(8,128)(2,1)S(1)}, bf16[64,1408]{1,0:T(8,128)(2,1)S(1)}, u32[]{:S(2)}, u32[]{:S(2)}) collective-permute-start(bf16[64,1408]{1,0:T(8,128)(2,1)S(1)} %get-tuple-element.27), channel_id=1, source_target_pairs={{0,6},{1,7},{2,4},{3,5},{4,2},{5,3},{6,0},{7,1},{8,14},{9,15},{10,... | collective-permute-start | bytes 540680 | tf_op jit(solution)/shard_map/ppermute | solution.py:313
  7.5 1.1 collective-permute-start.1
  8.7 0.8 collective-permute-start.2
  9.5 2.0 %collective-permute-start.3 = (bf16[64,1408]{1,0:T(8,128)(2,1)S(1)}, bf16[64,1408]{1,0:T(8,128)(2,1)S(1)}, u32[]{:S(2)}, u32[]{:S(2)}) collective-permute-start(bf16[64,1408]{1,0:T(8,128)(2,1)S(1)} %get-tuple-element.30), channel_id=1, source_target_pairs={{0,5},{1,4},{2,7},{3,6},{4,1},{5,0},{6,3},{7,2},{8,13},{9,12},{10,... | collective-permute-start | bytes 540680 | tf_op jit(solution)/shard_map/ppermute | solution.py:313
  11.4 1.4 collective-permute-start.4
  12.9 16.3 %collective-permute-start.5 = (bf16[64,1408]{1,0:T(8,128)(2,1)S(1)}, bf16[64,1408]{1,0:T(8,128)(2,1)S(1)}, u32[]{:S(2)}, u32[]{:S(2)}) collective-permute-start(bf16[64,1408]{1,0:T(8,128)(2,1)S(1)} %get-tuple-element.32), channel_id=1, source_target_pairs={{0,3},{1,2},{2,1},{3,0},{4,7},{5,6},{6,5},{7,4},{8,11},{9,10},{10,... | collective-permute-start | bytes 540680 | tf_op jit(solution)/shard_map/ppermute | solution.py:313
  29.7 5.8 %collective-permute-done.2.refs_2_ = bf16[64,1408]{1,0:T(8,128)(2,1)S(1)} collective-permute-done((bf16[64,1408]{1,0:T(8,128)(2,1)S(1)}, bf16[64,1408]{1,0:T(8,128)(2,1)S(1)}, u32[]{:S(2)}, u32[]{:S(2)}) %collective-permute-start.2) | collective-permute-done | bytes 180256 | tf_op jit(solution)/shard_map/ppermute | solution.py:313
  35.5 3.9 %collective-permute-done.3.refs_3_ = bf16[64,1408]{1,0:T(8,128)(2,1)S(1)} collective-permute-done((bf16[64,1408]{1,0:T(8,128)(2,1)S(1)}, bf16[64,1408]{1,0:T(8,128)(2,1)S(1)}, u32[]{:S(2)}, u32[]{:S(2)}) %collective-permute-start.3) | collective-permute-done | bytes 180256 | tf_op jit(solution)/shard_map/ppermute | solution.py:313
  39.3 0.9 collective-permute-done.5.refs_5_
  40.3 2.0 %center.1.refs_0_.refs_2_.refs_4_.refs_6_ = bf16[1344,512]{1,0:T(8,128)(2,1)S(1)} custom-call(bf16[64,1408]{1,0:T(8,128)(2,1)S(1)} %collective-permute-done.refs_0_, bf16[64,1408]{1,0:T(8,128)(2,1)S(1)} %collective-permute-done.1.refs_1_, bf16[64,1408]{1,0:T(8,128)(2,1)S(1)} %collective-permute-done.2.refs_2_, ...), custom_call_target="tpu_custom_call" | custom-call | tf_op jit(solution)/shard_map/center/pallas_call | solution.py:122
  42.3 0.7 collective-permute-start.10
  43.1 1.6 collective-permute-start.11
  45.2 2.6 %collective-permute-start.9 = (bf16[1344,512]{1,0:T(8,128)(2,1)S(1)}, bf16[1344,512]{1,0:T(8,128)(2,1)S(1)}, u32[]{:S(2)}, u32[]{:S(2)}) collective-permute-start(bf16[1344,512]{1,0:T(8,128)(2,1)S(1)} %center.1.refs_0_.refs_2_.refs_4_.refs_6_), channel_id=1, source_target_pairs={{0,2},{1,3},{2,0},{3,1},{4,6},{5,7},{6,4},{7,5},{8,10},{9,11},{10,... | collective-permute-start | bytes 4128776 | tf_op jit(solution)/shard_map/ppermute | solution.py:313
  47.8 8.0 %tiles.5 = (f32[4,1344,10752]{2,1,0:T(8,128)}, bf16[2688,512]{1,0:T(8,128)(2,1)}) custom-call(bf16[1344,512]{1,0:T(8,128)(2,1)S(1)} %center.1.refs_0_.refs_2_.refs_4_.refs_6_, bf16[1344,512]{1,0:T(8,128)(2,1)S(1)} %collective-permute-done.7.refs_1_, bf16[1344,512]{1,0:T(8,128)(2,1)S(1)} %center.1.refs_0_.refs_2_.refs_4_.refs_6_), custom_call_target="tpu_custom_call" | custom-call | flops 3523215360 | bytes 13762560 | tf_op jit(solution)/shard_map/tiles/pallas_call | solution.py:289
  55.8 20.0 %collective-permute-done.11.refs_2_ = bf16[1344,512]{1,0:T(8,128)(2,1)} collective-permute-done((bf16[1344,512]{1,0:T(8,128)(2,1)S(1)}, bf16[1344,512]{1,0:T(8,128)(2,1)}, u32[]{:S(2)}, u32[]{:S(2)}) %collective-permute-start.11) | collective-permute-done | bytes 1376288 | tf_op jit(solution)/shard_map/ppermute | solution.py:313
  75.8 1.1 collective-permute-done.8.refs_5_
  77.0 1.1 copy-done.2
  78.1 4.6 %collective-permute-start.14 = (bf16[1344,512]{1,0:T(8,128)(2,1)S(1)}, bf16[1344,512]{1,0:T(8,128)(2,1)S(1)}, u32[]{:S(2)}, u32[]{:S(2)}) collective-permute-start(bf16[1344,512]{1,0:T(8,128)(2,1)S(1)} %center.1.refs_0_.refs_2_.refs_4_.refs_6_), channel_id=1, source_target_pairs={{0,6},{6,0},{1,7},{7,1},{8,14},{14,8},{9,15},{15,9},{16,22},{22,16... | collective-permute-start | bytes 4128776 | tf_op jit(solution)/shard_map/ppermute | solution.py:339
  83.4 1.3 copy-done.1
  84.8 1.3 copy-done.3
  86.1 27.7 %tiles.6 = (f32[4,1344,10752]{2,1,0:T(8,128)}, bf16[5376,512]{1,0:T(8,128)(2,1)S(1)}) custom-call(bf16[1344,512]{1,0:T(8,128)(2,1)S(1)} %center.1.refs_0_.refs_2_.refs_4_.refs_6_, bf16[1344,512]{1,0:T(8,128)(2,1)S(1)} %copy-done.1, bf16[1344,512]{1,0:T(8,128)(2,1)} %collective-permute-done.11.refs_2_, ...), custom_call_target="tpu_custom_call", output_to_operand_aliasing={{0}: (8, {})} | custom-call | flops 18320719872 | bytes 71565312 | tf_op jit(solution)/shard_map/tiles/pallas_call | solution.py:289
  114.4 0.7 collective-permute-done.13.refs_2_
  115.3 0.7 collective-permute-start.16
  115.9 2.0 %collective-permute-start.15 = (bf16[672,512]{1,0:T(8,128)(2,1)S(1)}, bf16[672,512]{1,0:T(8,128)(2,1)S(1)}, u32[]{:S(2)}, u32[]{:S(2)}) collective-permute-start(bf16[672,512]{1,0:T(8,128)(2,1)S(1)} %get-tuple-element.50.refs_3_.refs_1_), channel_id=1, source_target_pairs={{0,2},{1,3},{2,0},{3,1},{4,6},{5,7},{6,4},{7,5},{8,10},{9,11},{10,... | collective-permute-start | bytes 2064392 | tf_op jit(solution)/shard_map/ppermute | solution.py:313
  118.0 1.4 collective-permute-start.20
  119.4 20.9 %tiles.7.refs_7_ = f32[4,1344,10752]{2,1,0:T(8,128)} custom-call(bf16[5376,512]{1,0:T(8,128)(2,1)S(1)} %get-tuple-element.40.refs_0_, bf16[1344,512]{1,0:T(8,128)(2,1)S(1)} %collective-permute-done.9.refs_7_.refs_1_, bf16[1344,512]{1,0:T(8,128)(2,1)S(1)} %collective-permute-done.13.refs_2_, ...), custom_call_target="tpu_custom_call", output_to_operand_aliasing={{}: (5, {})} | custom-call | flops 14797504512 | bytes 57802752 | tf_op jit(solution)/shard_map/tiles/pallas_call | solution.py:289
  140.3 7.1 %collective-permute-done.15.refs_5_.refs_1_ = bf16[672,512]{1,0:T(8,128)(2,1)S(1)} collective-permute-done((bf16[672,512]{1,0:T(8,128)(2,1)S(1)}, bf16[672,512]{1,0:T(8,128)(2,1)S(1)}, u32[]{:S(2)}, u32[]{:S(2)}) %collective-permute-start.15) | collective-permute-done | bytes 688160 | tf_op jit(solution)/shard_map/ppermute | solution.py:313
  147.4 1.1 collective-permute-start.18
  148.8 20.9 %tiles.8.refs_5_ = f32[4,1344,10752]{2,1,0:T(8,128)} custom-call(bf16[5376,512]{1,0:T(8,128)(2,1)S(1)} %get-tuple-element.40.refs_0_, bf16[672,512]{1,0:T(8,128)(2,1)S(1)} %get-tuple-element.50.refs_3_.refs_1_, bf16[672,512]{1,0:T(8,128)(2,1)S(1)} %get-tuple-element.49.refs_4_.refs_2_, ...), custom_call_target="tpu_custom_call", output_to_operand_aliasing={{}: (7, {})} | custom-call | flops 14797504512 | bytes 57802752 | tf_op jit(solution)/shard_map/tiles/pallas_call | solution.py:289
  169.8 12.2 %tiles.9 = f32[4,1344,10752]{2,1,0:T(8,128)} custom-call(bf16[5376,512]{1,0:T(8,128)(2,1)S(1)} %get-tuple-element.40.refs_0_, bf16[672,512]{1,0:T(8,128)(2,1)S(1)} %collective-permute-done.15.refs_5_.refs_1_, bf16[672,512]{1,0:T(8,128)(2,1)S(1)} %collective-permute-done.17.refs_6_.refs_2_, ...), custom_call_target="tpu_custom_call", output_to_operand_aliasing={{}: (5, {})} | custom-call | flops 7751073792 | bytes 30277632 | tf_op jit(solution)/shard_map/tiles/pallas_call | solution.py:289
  (34 shorter events, 3.3 us)
Async XLA Ops:
  0.0 1.3 copy-start.4
  1.3 0.7 copy-start.5
  2.4 10.4 %collective-permute-start = (bf16[64,1408]{1,0:T(8,128)(2,1)S(1)}, bf16[64,1408]{1,0:T(8,128)(2,1)S(1)}, u32[]{:S(2)}, u32[]{:S(2)}) collective-permute-start(bf16[64,1408]{1,0:T(8,128)(2,1)S(1)} %get-tuple-element.27), channel_id=1, source_target_pairs={{0,6},{1,7},{2,4},{3,5},{4,2},{5,3},{6,0},{7,1},{8,14},{9,15},{10,... | collective-permute-start | bytes 540680 | tf_op jit(solution)/shard_map/ppermute | solution.py:313
  7.5 21.6 %collective-permute-start.1 = (bf16[64,1408]{1,0:T(8,128)(2,1)S(1)}, bf16[64,1408]{1,0:T(8,128)(2,1)S(1)}, u32[]{:S(2)}, u32[]{:S(2)}) collective-permute-start(bf16[64,1408]{1,0:T(8,128)(2,1)S(1)} %get-tuple-element.28), channel_id=1, source_target_pairs={{0,7},{1,6},{2,5},{3,4},{4,3},{5,2},{6,1},{7,0},{8,15},{9,14},{10,... | collective-permute-start | bytes 540680 | tf_op jit(solution)/shard_map/ppermute | solution.py:313
  8.7 26.8 %collective-permute-start.2 = (bf16[64,1408]{1,0:T(8,128)(2,1)S(1)}, bf16[64,1408]{1,0:T(8,128)(2,1)S(1)}, u32[]{:S(2)}, u32[]{:S(2)}) collective-permute-start(bf16[64,1408]{1,0:T(8,128)(2,1)S(1)} %get-tuple-element.29), channel_id=1, source_target_pairs={{0,4},{1,5},{2,6},{3,7},{4,0},{5,1},{6,2},{7,3},{8,12},{9,13},{10,... | collective-permute-start | bytes 540680 | tf_op jit(solution)/shard_map/ppermute | solution.py:313
  9.5 29.8 %collective-permute-start.3 = (bf16[64,1408]{1,0:T(8,128)(2,1)S(1)}, bf16[64,1408]{1,0:T(8,128)(2,1)S(1)}, u32[]{:S(2)}, u32[]{:S(2)}) collective-permute-start(bf16[64,1408]{1,0:T(8,128)(2,1)S(1)} %get-tuple-element.30), channel_id=1, source_target_pairs={{0,5},{1,4},{2,7},{3,6},{4,1},{5,0},{6,3},{7,2},{8,13},{9,12},{10,... | collective-permute-start | bytes 540680 | tf_op jit(solution)/shard_map/ppermute | solution.py:313
  11.4 27.9 %collective-permute-start.4 = (bf16[64,1408]{1,0:T(8,128)(2,1)S(1)}, bf16[64,1408]{1,0:T(8,128)(2,1)S(1)}, u32[]{:S(2)}, u32[]{:S(2)}) collective-permute-start(bf16[64,1408]{1,0:T(8,128)(2,1)S(1)} %get-tuple-element.31), channel_id=1, source_target_pairs={{0,2},{1,3},{2,0},{3,1},{4,6},{5,7},{6,4},{7,5},{8,10},{9,11},{10,... | collective-permute-start | bytes 540680 | tf_op jit(solution)/shard_map/ppermute | solution.py:313
  12.9 27.4 %collective-permute-start.5 = (bf16[64,1408]{1,0:T(8,128)(2,1)S(1)}, bf16[64,1408]{1,0:T(8,128)(2,1)S(1)}, u32[]{:S(2)}, u32[]{:S(2)}) collective-permute-start(bf16[64,1408]{1,0:T(8,128)(2,1)S(1)} %get-tuple-element.32), channel_id=1, source_target_pairs={{0,3},{1,2},{2,1},{3,0},{4,7},{5,6},{6,5},{7,4},{8,11},{9,10},{10,... | collective-permute-start | bytes 540680 | tf_op jit(solution)/shard_map/ppermute | solution.py:313
  29.1 11.1 %collective-permute-start.6 = (bf16[64,1408]{1,0:T(8,128)(2,1)S(1)}, bf16[64,1408]{1,0:T(8,128)(2,1)S(1)}, u32[]{:S(2)}, u32[]{:S(2)}) collective-permute-start(bf16[64,1408]{1,0:T(8,128)(2,1)S(1)} %get-tuple-element.33), channel_id=1, source_target_pairs={{0,1},{1,0},{2,3},{3,2},{4,5},{5,4},{6,7},{7,6},{8,9},{9,8},{10,11... | collective-permute-start | bytes 540680 | tf_op jit(solution)/shard_map/ppermute | solution.py:313
  42.3 5.5 %collective-permute-start.7 = (bf16[1344,512]{1,0:T(8,128)(2,1)S(1)}, bf16[1344,512]{1,0:T(8,128)(2,1)S(1)}, u32[]{:S(2)}, u32[]{:S(2)}) collective-permute-start(bf16[1344,512]{1,0:T(8,128)(2,1)S(1)} %center.1.refs_0_.refs_2_.refs_4_.refs_6_), channel_id=1, source_target_pairs={{0,8},{8,0},{16,24},{24,16},{1,9},{9,1},{17,25},{25,17},{2,10},{10... | collective-permute-start | bytes 4128776 | tf_op jit(solution)/shard_map/ppermute | solution.py:313
  42.3 13.4 %collective-permute-start.10 = (bf16[1344,512]{1,0:T(8,128)(2,1)S(1)}, bf16[1344,512]{1,0:T(8,128)(2,1)S(1)}, u32[]{:S(2)}, u32[]{:S(2)}) collective-permute-start(bf16[1344,512]{1,0:T(8,128)(2,1)S(1)} %center.1.refs_0_.refs_2_.refs_4_.refs_6_), channel_id=1, source_target_pairs={{2,4},{4,2},{3,5},{5,3},{10,12},{12,10},{11,13},{13,11},{18,20},{2... | collective-permute-start | bytes 4128776 | tf_op jit(solution)/shard_map/ppermute | solution.py:336
  43.1 32.7 %collective-permute-start.11 = (bf16[1344,512]{1,0:T(8,128)(2,1)S(1)}, bf16[1344,512]{1,0:T(8,128)(2,1)}, u32[]{:S(2)}, u32[]{:S(2)}) collective-permute-start(bf16[1344,512]{1,0:T(8,128)(2,1)S(1)} %center.1.refs_0_.refs_2_.refs_4_.refs_6_), channel_id=1, source_target_pairs={{0,16},{8,24},{16,0},{24,8},{1,17},{9,25},{17,1},{25,9},{2,18},{10... | collective-permute-start | bytes 4128776 | tf_op jit(solution)/shard_map/ppermute | solution.py:313
  44.7 32.3 %collective-permute-start.8 = (bf16[1344,512]{1,0:T(8,128)(2,1)S(1)}, bf16[1344,512]{1,0:T(8,128)(2,1)S(1)}, u32[]{:S(2)}, u32[]{:S(2)}) collective-permute-start(bf16[1344,512]{1,0:T(8,128)(2,1)S(1)} %center.1.refs_0_.refs_2_.refs_4_.refs_6_), channel_id=1, source_target_pairs={{0,1},{1,0},{2,3},{3,2},{4,5},{5,4},{6,7},{7,6},{8,9},{9,8},{10,11... | collective-permute-start | bytes 4128776 | tf_op jit(solution)/shard_map/ppermute | solution.py:313
  45.2 32.9 %collective-permute-start.9 = (bf16[1344,512]{1,0:T(8,128)(2,1)S(1)}, bf16[1344,512]{1,0:T(8,128)(2,1)S(1)}, u32[]{:S(2)}, u32[]{:S(2)}) collective-permute-start(bf16[1344,512]{1,0:T(8,128)(2,1)S(1)} %center.1.refs_0_.refs_2_.refs_4_.refs_6_), channel_id=1, source_target_pairs={{0,2},{1,3},{2,0},{3,1},{4,6},{5,7},{6,4},{7,5},{8,10},{9,11},{10,... | collective-permute-start | bytes 4128776 | tf_op jit(solution)/shard_map/ppermute | solution.py:313
  47.8 8.0 %copy-start = (bf16[1344,512]{1,0:T(8,128)(2,1)}, bf16[1344,512]{1,0:T(8,128)(2,1)S(1)}, u32[]{:S(2)}) copy-start(bf16[1344,512]{1,0:T(8,128)(2,1)S(1)} %collective-permute-done.7.refs_1_) | copy-start | bytes 4128772
  55.8 22.3 %copy-start.6 = (bf16[1344,512]{1,0:T(8,128)(2,1)}, bf16[1344,512]{1,0:T(8,128)(2,1)S(1)}, u32[]{:S(2)}) copy-start(bf16[1344,512]{1,0:T(8,128)(2,1)S(1)} %collective-permute-done.10) | copy-start | bytes 4128772
  77.0 1.1 copy-start.2
  78.1 5.3 %collective-permute-start.12 = (bf16[1344,512]{1,0:T(8,128)(2,1)}, bf16[1344,512]{1,0:T(8,128)(2,1)}, u32[]{:S(2)}, u32[]{:S(2)}) collective-permute-start(bf16[1344,512]{1,0:T(8,128)(2,1)} %collective-permute-done.11.refs_2_), channel_id=1, source_target_pairs={{0,8},{8,0},{16,24},{24,16},{1,9},{9,1},{17,25},{25,17},{2,10},{10... | collective-permute-start | bytes 4128776 | tf_op jit(solution)/shard_map/ppermute | solution.py:313
  78.1 36.3 %collective-permute-start.14 = (bf16[1344,512]{1,0:T(8,128)(2,1)S(1)}, bf16[1344,512]{1,0:T(8,128)(2,1)S(1)}, u32[]{:S(2)}, u32[]{:S(2)}) collective-permute-start(bf16[1344,512]{1,0:T(8,128)(2,1)S(1)} %center.1.refs_0_.refs_2_.refs_4_.refs_6_), channel_id=1, source_target_pairs={{0,6},{6,0},{1,7},{7,1},{8,14},{14,8},{9,15},{15,9},{16,22},{22,16... | collective-permute-start | bytes 4128776 | tf_op jit(solution)/shard_map/ppermute | solution.py:339
  82.8 32.3 %collective-permute-start.13 = (bf16[1344,512]{1,0:T(8,128)(2,1)S(1)}, bf16[1344,512]{1,0:T(8,128)(2,1)S(1)}, u32[]{:S(2)}, u32[]{:S(2)}) collective-permute-start(bf16[1344,512]{1,0:T(8,128)(2,1)S(1)} %collective-permute-done.9.refs_7_.refs_1_), channel_id=1, source_target_pairs={{0,1},{1,0},{2,3},{3,2},{4,5},{5,4},{6,7},{7,6},{8,9},{9,8},{10,11... | collective-permute-start | bytes 4128776 | tf_op jit(solution)/shard_map/ppermute | solution.py:313
  83.4 1.3 copy-start.1
  84.8 1.3 copy-start.3
  86.1 29.0 %copy-start.7 = (bf16[1344,512]{1,0:T(8,128)(2,1)S(1)}, bf16[1344,512]{1,0:T(8,128)(2,1)}, u32[]{:S(2)}) copy-start(bf16[1344,512]{1,0:T(8,128)(2,1)} %copy-done.6) | copy-start | bytes 4128772
  115.3 32.2 %collective-permute-start.16 = (bf16[672,512]{1,0:T(8,128)(2,1)S(1)}, bf16[672,512]{1,0:T(8,128)(2,1)S(1)}, u32[]{:S(2)}, u32[]{:S(2)}) collective-permute-start(bf16[672,512]{1,0:T(8,128)(2,1)S(1)} %get-tuple-element.49.refs_4_.refs_2_), channel_id=1, source_target_pairs={{0,1},{1,0},{2,3},{3,2},{4,5},{5,4},{6,7},{7,6},{8,9},{9,8},{10,11... | collective-permute-start | bytes 2064392 | tf_op jit(solution)/shard_map/ppermute | solution.py:313
  115.9 32.9 %collective-permute-start.17 = (bf16[672,512]{1,0:T(8,128)(2,1)S(1)}, bf16[672,512]{1,0:T(8,128)(2,1)S(1)}, u32[]{:S(2)}, u32[]{:S(2)}) collective-permute-start(bf16[672,512]{1,0:T(8,128)(2,1)S(1)} %get-tuple-element.49.refs_4_.refs_2_), channel_id=1, source_target_pairs={{0,2},{1,3},{2,0},{3,1},{4,6},{5,7},{6,4},{7,5},{8,10},{9,11},{10,... | collective-permute-start | bytes 2064392 | tf_op jit(solution)/shard_map/ppermute | solution.py:313
  115.9 31.5 %collective-permute-start.15 = (bf16[672,512]{1,0:T(8,128)(2,1)S(1)}, bf16[672,512]{1,0:T(8,128)(2,1)S(1)}, u32[]{:S(2)}, u32[]{:S(2)}) collective-permute-start(bf16[672,512]{1,0:T(8,128)(2,1)S(1)} %get-tuple-element.50.refs_3_.refs_1_), channel_id=1, source_target_pairs={{0,2},{1,3},{2,0},{3,1},{4,6},{5,7},{6,4},{7,5},{8,10},{9,11},{10,... | collective-permute-start | bytes 2064392 | tf_op jit(solution)/shard_map/ppermute | solution.py:313
  118.0 30.9 %collective-permute-start.20 = (bf16[672,512]{1,0:T(8,128)(2,1)S(1)}, bf16[672,512]{1,0:T(8,128)(2,1)S(1)}, u32[]{:S(2)}, u32[]{:S(2)}) collective-permute-start(bf16[672,512]{1,0:T(8,128)(2,1)S(1)} %get-tuple-element.50.refs_3_.refs_1_), channel_id=1, source_target_pairs={{0,1},{1,0},{2,3},{3,2},{4,5},{5,4},{6,7},{7,6},{8,9},{9,8},{10,11... | collective-permute-start | bytes 2064392 | tf_op jit(solution)/shard_map/ppermute | solution.py:313
  147.4 22.3 %collective-permute-start.18 = (bf16[672,512]{1,0:T(8,128)(2,1)S(1)}, bf16[672,512]{1,0:T(8,128)(2,1)S(1)}, u32[]{:S(2)}, u32[]{:S(2)}) collective-permute-start(bf16[672,512]{1,0:T(8,128)(2,1)S(1)} %collective-permute-done.15.refs_5_.refs_1_), channel_id=1, source_target_pairs={{0,1},{1,0},{2,3},{3,2},{4,5},{5,4},{6,7},{7,6},{8,9},{9,8},{10,11... | collective-permute-start | bytes 2064392 | tf_op jit(solution)/shard_map/ppermute | solution.py:313
  148.5 21.2 %collective-permute-start.19 = (bf16[672,512]{1,0:T(8,128)(2,1)S(1)}, bf16[672,512]{1,0:T(8,128)(2,1)S(1)}, u32[]{:S(2)}, u32[]{:S(2)}) collective-permute-start(bf16[672,512]{1,0:T(8,128)(2,1)S(1)} %collective-permute-done.16.refs_4_), channel_id=1, source_target_pairs={{0,2},{1,3},{2,0},{3,1},{4,6},{5,7},{6,4},{7,5},{8,10},{9,11},{10,... | collective-permute-start | bytes 2064392 | tf_op jit(solution)/shard_map/ppermute | solution.py:313

commit v4 on v3

--- a/solution.py
+++ b/solution.py
@@ -336,35 +336,40 @@
     z3_middle = lax.ppermute(own, "seq", [(2, 4), (4, 2), (3, 5), (5, 3)])
     y_own = flip(own, "blk", 2)
     core_own = flip(own, "blk", 1)
-    z3_outer = lax.ppermute(own, "seq", [(0, 6), (6, 0), (1, 7), (7, 1)])
     out, _ = tiles(None, out_shape, [own, core_own], [(FIRST, 0, [own], [], (0, 2))])
     x_own, z1, z3_middle, y_own, out = wait_all(x_own, z1, z3_middle, y_own, out)
+    half = stripe // 2
+    parts_of = (slice(0, half), slice(half, stripe))
     x_z1 = flip(z1, "seq", 1)
     core_y = flip(y_own, "blk", 1)
+    outer_pairs = [(0, 6), (6, 0), (1, 7), (7, 1)]
+    z3_outer = [lax.ppermute(own[rows], "seq", outer_pairs) for rows in parts_of]
     every = (0, 4)
     out, left = tiles(
         out,
         out_shape,
         [own, core_own, y_own, core_y],
+        [(SECOND, 0, [own], [x_own], every), (FIRST, 1, [z1], [], every)],
+    )
+    out, z3_outer[0] = wait_all(out, z3_outer[0])
+    z3 = [jnp.where(middle, z3_middle[parts_of[0]], z3_outer[0])]
+    x_z3, z2 = [flip(z3[0], "seq", 1)], [flip(z3[0], "seq", 2)]
+    out, x_z1, z3_outer[1] = wait_all(out, x_z1, z3_outer[1])
+    z3.append(jnp.where(middle, z3_middle[parts_of[1]], z3_outer[1]))
+    x_z3.append(flip(z3[1], "seq", 1))
+    z2.append(flip(z3[1], "seq", 2))
+    out = tiles(
+        out,
+        out_shape,
+        left,
         [
-            (SECOND, 0, [own], [x_own], every),
+            (SECOND, 1, [z1], [x_z1], every),
+            (FIRST, 3, z3, [], every),
             (FIRST, 0, [own], [], (2, 4)),
-            (FIRST, 1, [z1], [], every),
         ],
     )
-    out, x_z1, z3_outer = wait_all(out, x_z1, z3_outer)
-    half = stripe // 2
-    z3 = [
-        jnp.where(middle, z3_middle[rows], z3_outer[rows])
-        for rows in (slice(0, half), slice(half, stripe))
-    ]
-    x_z3_low = flip(z3[1], "seq", 1)
-    z2_top = flip(z3[0], "seq", 2)
-    x_z3 = [flip(z3[0], "seq", 1), x_z3_low]
-    z2 = [z2_top, flip(z3[1], "seq", 2)]
-    out = tiles(out, out_shape, left, [(SECOND, 1, [z1], [x_z1], every), (FIRST, 3, z3, [], every)])
-    out, z2[0], x_z3[1] = wait_all(out, z2[0], x_z3[1])
-    x_z2 = [flip(z2[0], "seq", 1), flip(x_z3[1], "seq", 2)]
+    out, x_z3[0], z2[1] = wait_all(out, x_z3[0], z2[1])
+    x_z2 = [flip(x_z3[0], "seq", 2), flip(z2[1], "seq", 1)]
     out = tiles(out, out_shape, left, [(SECOND, 3, z3, x_z3, every), (FIRST, 2, z2, [], every)])
     return tiles(out, out_shape, left, [(SECOND, 2, z2, x_z2, every)])
 

time: 182 us -> 185 us (1.016)
  starting transfers between devices: 43.5 us -> 47.1 us
  local copies, waits for them, and re-layouts: 5.81 us -> 3.22 us
    ppermute x1 -> x2, waiting for transfers between devices: 0.61 us -> 4.03 us  [fast_body(): lax.ppermute(own[rows], 'seq', outer_pairs)]
    ppermute x1 -> x2, starting transfers between devices: 4.64 us -> 7.9 us  [fast_body(): lax.ppermute(own[rows], 'seq', outer_pairs)]
    unnamed x16, local copies, waits for them, and re-layouts: 5.81 us -> 3.13 us
  transfers between devices with their start and end apart: 21 -> 22, of which waited for: 8 -> 8; matrix products, arithmetic and copies ran while one was open for 0% -> 0% of each run, Pallas kernels for 43% -> 42%
where the time goes in v4:
time: 185 us
  Pallas kernels  91.9 us (50%)
  starting transfers between devices  47.1 us (25%)
  waiting for transfers between devices  42.1 us (23%)
  local copies, waits for them, and re-layouts  3.22 us (2%)
    pallas_call x5, Pallas kernels, tiles(): pl.pallas_call(functools.partial(tiles_kernel, forms, joining, out is not...  89.5 us
    ppermute x19, starting transfers between devices, flip(): lax.ppermute(value, axis, [(source, source ^ bits) for source in range(co...  38.4 us
    ppermute x19, waiting for transfers between devices, flip(): lax.ppermute(value, axis, [(source, source ^ bits) for source in range(co...  38.1 us
    ppermute x2, starting transfers between devices, fast_body(): lax.ppermute(own[rows], 'seq', outer_pairs)  7.9 us
    ppermute x2, waiting for transfers between devices, fast_body(): lax.ppermute(own[rows], 'seq', outer_pairs)  4.03 us
  transfers between devices with their start and end apart: 22, of which 8 were waited for; matrix products, arithmetic and copies ran while one was open for 0% of the time, Pallas kernels for 42%

profile of v4, /device:TPU:0, one launch (start us, length us, event | category | flops | bytes accessed | tf_op | source)
XLA Modules:
  0.0 184.7 jit_solution(9429222461733820140)
XLA Ops:
  0.0 1.3 copy-done.4
  2.4 5.1 %collective-permute-start = (bf16[64,1408]{1,0:T(8,128)(2,1)S(1)}, bf16[64,1408]{1,0:T(8,128)(2,1)S(1)}, u32[]{:S(2)}, u32[]{:S(2)}) collective-permute-start(bf16[64,1408]{1,0:T(8,128)(2,1)S(1)} %get-tuple-element.29), channel_id=1, source_target_pairs={{0,6},{1,7},{2,4},{3,5},{4,2},{5,3},{6,0},{7,1},{8,14},{9,15},{10,... | collective-permute-start | bytes 540680 | tf_op jit(solution)/shard_map/ppermute | solution.py:313
  7.5 1.1 collective-permute-start.1
  8.7 0.8 collective-permute-start.2
  9.5 2.0 %collective-permute-start.3 = (bf16[64,1408]{1,0:T(8,128)(2,1)S(1)}, bf16[64,1408]{1,0:T(8,128)(2,1)S(1)}, u32[]{:S(2)}, u32[]{:S(2)}) collective-permute-start(bf16[64,1408]{1,0:T(8,128)(2,1)S(1)} %get-tuple-element.32), channel_id=1, source_target_pairs={{0,5},{1,4},{2,7},{3,6},{4,1},{5,0},{6,3},{7,2},{8,13},{9,12},{10,... | collective-permute-start | bytes 540680 | tf_op jit(solution)/shard_map/ppermute | solution.py:313
  11.4 1.4 collective-permute-start.4
  12.9 16.3 %collective-permute-start.5 = (bf16[64,1408]{1,0:T(8,128)(2,1)S(1)}, bf16[64,1408]{1,0:T(8,128)(2,1)S(1)}, u32[]{:S(2)}, u32[]{:S(2)}) collective-permute-start(bf16[64,1408]{1,0:T(8,128)(2,1)S(1)} %get-tuple-element.34), channel_id=1, source_target_pairs={{0,3},{1,2},{2,1},{3,0},{4,7},{5,6},{6,5},{7,4},{8,11},{9,10},{10,... | collective-permute-start | bytes 540680 | tf_op jit(solution)/shard_map/ppermute | solution.py:313
  29.7 5.8 %collective-permute-done.2.refs_2_ = bf16[64,1408]{1,0:T(8,128)(2,1)S(1)} collective-permute-done((bf16[64,1408]{1,0:T(8,128)(2,1)S(1)}, bf16[64,1408]{1,0:T(8,128)(2,1)S(1)}, u32[]{:S(2)}, u32[]{:S(2)}) %collective-permute-start.2) | collective-permute-done | bytes 180256 | tf_op jit(solution)/shard_map/ppermute | solution.py:313
  35.5 3.9 %collective-permute-done.3.refs_3_ = bf16[64,1408]{1,0:T(8,128)(2,1)S(1)} collective-permute-done((bf16[64,1408]{1,0:T(8,128)(2,1)S(1)}, bf16[64,1408]{1,0:T(8,128)(2,1)S(1)}, u32[]{:S(2)}, u32[]{:S(2)}) %collective-permute-start.3) | collective-permute-done | bytes 180256 | tf_op jit(solution)/shard_map/ppermute | solution.py:313
  39.3 0.9 collective-permute-done.5.refs_5_
  40.3 2.0 %center.1.refs_0_.refs_2_.refs_4_.refs_5_ = bf16[1344,512]{1,0:T(8,128)(2,1)S(1)} custom-call(bf16[64,1408]{1,0:T(8,128)(2,1)S(1)} %collective-permute-done.refs_0_, bf16[64,1408]{1,0:T(8,128)(2,1)S(1)} %collective-permute-done.1.refs_1_, bf16[64,1408]{1,0:T(8,128)(2,1)S(1)} %collective-permute-done.2.refs_2_, ...), custom_call_target="tpu_custom_call" | custom-call | tf_op jit(solution)/shard_map/center/pallas_call | solution.py:122
  42.3 0.7 collective-permute-start.10
  43.1 1.6 collective-permute-start.11
  45.2 2.6 %collective-permute-start.9 = (bf16[1344,512]{1,0:T(8,128)(2,1)S(1)}, bf16[1344,512]{1,0:T(8,128)(2,1)S(1)}, u32[]{:S(2)}, u32[]{:S(2)}) collective-permute-start(bf16[1344,512]{1,0:T(8,128)(2,1)S(1)} %center.1.refs_0_.refs_2_.refs_4_.refs_5_), channel_id=1, source_target_pairs={{0,2},{1,3},{2,0},{3,1},{4,6},{5,7},{6,4},{7,5},{8,10},{9,11},{10,... | collective-permute-start | bytes 4128776 | tf_op jit(solution)/shard_map/ppermute | solution.py:313
  47.8 8.0 %tiles.5 = (f32[4,1344,10752]{2,1,0:T(8,128)}, bf16[2688,512]{1,0:T(8,128)(2,1)}) custom-call(bf16[1344,512]{1,0:T(8,128)(2,1)S(1)} %center.1.refs_0_.refs_2_.refs_4_.refs_5_, bf16[1344,512]{1,0:T(8,128)(2,1)S(1)} %collective-permute-done.7.refs_1_, bf16[1344,512]{1,0:T(8,128)(2,1)S(1)} %center.1.refs_0_.refs_2_.refs_4_.refs_5_), custom_call_target="tpu_custom_call" | custom-call | flops 3523215360 | bytes 13762560 | tf_op jit(solution)/shard_map/tiles/pallas_call | solution.py:289
  55.8 20.1 %collective-permute-done.11.refs_2_ = bf16[1344,512]{1,0:T(8,128)(2,1)} collective-permute-done((bf16[1344,512]{1,0:T(8,128)(2,1)S(1)}, bf16[1344,512]{1,0:T(8,128)(2,1)}, u32[]{:S(2)}, u32[]{:S(2)}) %collective-permute-start.11) | collective-permute-done | bytes 1376288 | tf_op jit(solution)/shard_map/ppermute | solution.py:313
  75.8 1.1 collective-permute-done.8.refs_5_
  77.0 1.1 copy-done.2
  78.2 4.8 %collective-permute-start.13 = (bf16[672,512]{1,0:T(8,128)(2,1)S(1)}, bf16[672,512]{1,0:T(8,128)(2,1)S(1)}, u32[]{:S(2)}, u32[]{:S(2)}) collective-permute-start(bf16[672,512]{1,0:T(8,128)(2,1)S(1)} %get-tuple-element.56), channel_id=1, source_target_pairs={{0,6},{6,0},{1,7},{7,1},{8,14},{14,8},{9,15},{15,9},{16,22},{22,16... | collective-permute-start | bytes 2064392 | tf_op jit(solution)/shard_map/ppermute | solution.py:346
  83.0 3.1 %collective-permute-start.16 = (bf16[672,512]{1,0:T(8,128)(2,1)S(1)}, bf16[672,512]{1,0:T(8,128)(2,1)S(1)}, u32[]{:S(2)}, u32[]{:S(2)}) collective-permute-start(bf16[672,512]{1,0:T(8,128)(2,1)S(1)} %get-tuple-element.55), channel_id=1, source_target_pairs={{0,6},{6,0},{1,7},{7,1},{8,14},{14,8},{9,15},{15,9},{16,22},{22,16... | collective-permute-start | bytes 2064392 | tf_op jit(solution)/shard_map/ppermute | solution.py:346
  86.2 1.4 collective-permute-start.15
  87.5 23.0 %tiles.6 = (f32[4,1344,10752]{2,1,0:T(8,128)}, bf16[5376,512]{1,0:T(8,128)(2,1)S(1)}) custom-call(bf16[1344,512]{1,0:T(8,128)(2,1)S(1)} %center.1.refs_0_.refs_2_.refs_4_.refs_5_, bf16[1344,512]{1,0:T(8,128)(2,1)S(1)} %copy-done.1, bf16[1344,512]{1,0:T(8,128)(2,1)} %collective-permute-done.11.refs_2_, ...), custom_call_target="tpu_custom_call", output_to_operand_aliasing={{0}: (7, {})} | custom-call | flops 14797504512 | bytes 57802752 | tf_op jit(solution)/shard_map/tiles/pallas_call | solution.py:289
  110.6 4.0 %collective-permute-done.16 = bf16[672,512]{1,0:T(8,128)(2,1)S(1)} collective-permute-done((bf16[672,512]{1,0:T(8,128)(2,1)S(1)}, bf16[672,512]{1,0:T(8,128)(2,1)S(1)}, u32[]{:S(2)}, u32[]{:S(2)}) %collective-permute-start.16) | collective-permute-done | bytes 688160 | tf_op jit(solution)/shard_map/ppermute | solution.py:346
  114.6 3.6 %collective-permute-done.15.refs_2_ = bf16[1344,512]{1,0:T(8,128)(2,1)S(1)} collective-permute-done((bf16[1344,512]{1,0:T(8,128)(2,1)S(1)}, bf16[1344,512]{1,0:T(8,128)(2,1)S(1)}, u32[]{:S(2)}, u32[]{:S(2)}) %collective-permute-start.15) | collective-permute-done | bytes 1376288 | tf_op jit(solution)/shard_map/ppermute | solution.py:313
  118.4 1.4 collective-permute-start.17
  119.8 2.0 %collective-permute-start.18 = (bf16[672,512]{1,0:T(8,128)(2,1)S(1)}, bf16[672,512]{1,0:T(8,128)(2,1)S(1)}, u32[]{:S(2)}, u32[]{:S(2)}) collective-permute-start(bf16[672,512]{1,0:T(8,128)(2,1)S(1)} %get-tuple-element.53.refs_4_.refs_2_), channel_id=1, source_target_pairs={{0,2},{1,3},{2,0},{3,1},{4,6},{5,7},{6,4},{7,5},{8,10},{9,11},{10,... | collective-permute-start | bytes 2064392 | tf_op jit(solution)/shard_map/ppermute | solution.py:313
  121.8 0.7 collective-permute-start.21
  122.5 25.4 %tiles.7.refs_7_ = f32[4,1344,10752]{2,1,0:T(8,128)} custom-call(bf16[5376,512]{1,0:T(8,128)(2,1)S(1)} %get-tuple-element.42.refs_0_, bf16[1344,512]{1,0:T(8,128)(2,1)S(1)} %collective-permute-done.9.refs_6_.refs_1_, bf16[1344,512]{1,0:T(8,128)(2,1)S(1)} %collective-permute-done.15.refs_2_, ...), custom_call_target="tpu_custom_call", output_to_operand_aliasing={{}: (6, {})} | custom-call | flops 18320719872 | bytes 71565312 | tf_op jit(solution)/shard_map/tiles/pallas_call | solution.py:289
  147.9 2.7 %collective-permute-done.18.refs_6_.refs_2_ = bf16[672,512]{1,0:T(8,128)(2,1)S(1)} collective-permute-done((bf16[672,512]{1,0:T(8,128)(2,1)S(1)}, bf16[672,512]{1,0:T(8,128)(2,1)S(1)}, u32[]{:S(2)}, u32[]{:S(2)}) %collective-permute-start.18) | collective-permute-done | bytes 688160 | tf_op jit(solution)/shard_map/ppermute | solution.py:313
  150.9 0.7 collective-permute-start.20
  151.6 20.9 %tiles.8.refs_5_ = f32[4,1344,10752]{2,1,0:T(8,128)} custom-call(bf16[5376,512]{1,0:T(8,128)(2,1)S(1)} %get-tuple-element.42.refs_0_, bf16[672,512]{1,0:T(8,128)(2,1)S(1)} %get-tuple-element.54.refs_3_.refs_1_, bf16[672,512]{1,0:T(8,128)(2,1)S(1)} %get-tuple-element.53.refs_4_.refs_2_, ...), custom_call_target="tpu_custom_call", output_to_operand_aliasing={{}: (7, {})} | custom-call | flops 14797504512 | bytes 57802752 | tf_op jit(solution)/shard_map/tiles/pallas_call | solution.py:289
  172.5 12.2 %tiles.9 = f32[4,1344,10752]{2,1,0:T(8,128)} custom-call(bf16[5376,512]{1,0:T(8,128)(2,1)S(1)} %get-tuple-element.42.refs_0_, bf16[672,512]{1,0:T(8,128)(2,1)S(1)} %collective-permute-done.14.refs_5_.refs_1_, bf16[672,512]{1,0:T(8,128)(2,1)S(1)} %collective-permute-done.18.refs_6_.refs_2_, ...), custom_call_target="tpu_custom_call", output_to_operand_aliasing={{}: (5, {})} | custom-call | flops 7751073792 | bytes 30277632 | tf_op jit(solution)/shard_map/tiles/pallas_call | solution.py:289
  (37 shorter events, 2.8 us)
Async XLA Ops:
  0.0 1.3 copy-start.4
  1.3 0.7 copy-start.5
  2.4 10.4 %collective-permute-start = (bf16[64,1408]{1,0:T(8,128)(2,1)S(1)}, bf16[64,1408]{1,0:T(8,128)(2,1)S(1)}, u32[]{:S(2)}, u32[]{:S(2)}) collective-permute-start(bf16[64,1408]{1,0:T(8,128)(2,1)S(1)} %get-tuple-element.29), channel_id=1, source_target_pairs={{0,6},{1,7},{2,4},{3,5},{4,2},{5,3},{6,0},{7,1},{8,14},{9,15},{10,... | collective-permute-start | bytes 540680 | tf_op jit(solution)/shard_map/ppermute | solution.py:313
  7.5 21.6 %collective-permute-start.1 = (bf16[64,1408]{1,0:T(8,128)(2,1)S(1)}, bf16[64,1408]{1,0:T(8,128)(2,1)S(1)}, u32[]{:S(2)}, u32[]{:S(2)}) collective-permute-start(bf16[64,1408]{1,0:T(8,128)(2,1)S(1)} %get-tuple-element.30), channel_id=1, source_target_pairs={{0,7},{1,6},{2,5},{3,4},{4,3},{5,2},{6,1},{7,0},{8,15},{9,14},{10,... | collective-permute-start | bytes 540680 | tf_op jit(solution)/shard_map/ppermute | solution.py:313
  8.7 26.8 %collective-permute-start.2 = (bf16[64,1408]{1,0:T(8,128)(2,1)S(1)}, bf16[64,1408]{1,0:T(8,128)(2,1)S(1)}, u32[]{:S(2)}, u32[]{:S(2)}) collective-permute-start(bf16[64,1408]{1,0:T(8,128)(2,1)S(1)} %get-tuple-element.31), channel_id=1, source_target_pairs={{0,4},{1,5},{2,6},{3,7},{4,0},{5,1},{6,2},{7,3},{8,12},{9,13},{10,... | collective-permute-start | bytes 540680 | tf_op jit(solution)/shard_map/ppermute | solution.py:313
  9.5 29.8 %collective-permute-start.3 = (bf16[64,1408]{1,0:T(8,128)(2,1)S(1)}, bf16[64,1408]{1,0:T(8,128)(2,1)S(1)}, u32[]{:S(2)}, u32[]{:S(2)}) collective-permute-start(bf16[64,1408]{1,0:T(8,128)(2,1)S(1)} %get-tuple-element.32), channel_id=1, source_target_pairs={{0,5},{1,4},{2,7},{3,6},{4,1},{5,0},{6,3},{7,2},{8,13},{9,12},{10,... | collective-permute-start | bytes 540680 | tf_op jit(solution)/shard_map/ppermute | solution.py:313
  11.4 27.9 %collective-permute-start.4 = (bf16[64,1408]{1,0:T(8,128)(2,1)S(1)}, bf16[64,1408]{1,0:T(8,128)(2,1)S(1)}, u32[]{:S(2)}, u32[]{:S(2)}) collective-permute-start(bf16[64,1408]{1,0:T(8,128)(2,1)S(1)} %get-tuple-element.33), channel_id=1, source_target_pairs={{0,2},{1,3},{2,0},{3,1},{4,6},{5,7},{6,4},{7,5},{8,10},{9,11},{10,... | collective-permute-start | bytes 540680 | tf_op jit(solution)/shard_map/ppermute | solution.py:313
  12.9 27.4 %collective-permute-start.5 = (bf16[64,1408]{1,0:T(8,128)(2,1)S(1)}, bf16[64,1408]{1,0:T(8,128)(2,1)S(1)}, u32[]{:S(2)}, u32[]{:S(2)}) collective-permute-start(bf16[64,1408]{1,0:T(8,128)(2,1)S(1)} %get-tuple-element.34), channel_id=1, source_target_pairs={{0,3},{1,2},{2,1},{3,0},{4,7},{5,6},{6,5},{7,4},{8,11},{9,10},{10,... | collective-permute-start | bytes 540680 | tf_op jit(solution)/shard_map/ppermute | solution.py:313
  29.1 11.1 %collective-permute-start.6 = (bf16[64,1408]{1,0:T(8,128)(2,1)S(1)}, bf16[64,1408]{1,0:T(8,128)(2,1)S(1)}, u32[]{:S(2)}, u32[]{:S(2)}) collective-permute-start(bf16[64,1408]{1,0:T(8,128)(2,1)S(1)} %get-tuple-element.35), channel_id=1, source_target_pairs={{0,1},{1,0},{2,3},{3,2},{4,5},{5,4},{6,7},{7,6},{8,9},{9,8},{10,11... | collective-permute-start | bytes 540680 | tf_op jit(solution)/shard_map/ppermute | solution.py:313
  42.3 5.5 %collective-permute-start.7 = (bf16[1344,512]{1,0:T(8,128)(2,1)S(1)}, bf16[1344,512]{1,0:T(8,128)(2,1)S(1)}, u32[]{:S(2)}, u32[]{:S(2)}) collective-permute-start(bf16[1344,512]{1,0:T(8,128)(2,1)S(1)} %center.1.refs_0_.refs_2_.refs_4_.refs_5_), channel_id=1, source_target_pairs={{0,8},{8,0},{16,24},{24,16},{1,9},{9,1},{17,25},{25,17},{2,10},{10... | collective-permute-start | bytes 4128776 | tf_op jit(solution)/shard_map/ppermute | solution.py:313
  42.3 13.4 %collective-permute-start.10 = (bf16[1344,512]{1,0:T(8,128)(2,1)S(1)}, bf16[1344,512]{1,0:T(8,128)(2,1)S(1)}, u32[]{:S(2)}, u32[]{:S(2)}) collective-permute-start(bf16[1344,512]{1,0:T(8,128)(2,1)S(1)} %center.1.refs_0_.refs_2_.refs_4_.refs_5_), channel_id=1, source_target_pairs={{2,4},{4,2},{3,5},{5,3},{10,12},{12,10},{11,13},{13,11},{18,20},{2... | collective-permute-start | bytes 4128776 | tf_op jit(solution)/shard_map/ppermute | solution.py:336
  43.1 32.7 %collective-permute-start.11 = (bf16[1344,512]{1,0:T(8,128)(2,1)S(1)}, bf16[1344,512]{1,0:T(8,128)(2,1)}, u32[]{:S(2)}, u32[]{:S(2)}) collective-permute-start(bf16[1344,512]{1,0:T(8,128)(2,1)S(1)} %center.1.refs_0_.refs_2_.refs_4_.refs_5_), channel_id=1, source_target_pairs={{0,16},{8,24},{16,0},{24,8},{1,17},{9,25},{17,1},{25,9},{2,18},{10... | collective-permute-start | bytes 4128776 | tf_op jit(solution)/shard_map/ppermute | solution.py:313
  44.7 32.3 %collective-permute-start.8 = (bf16[1344,512]{1,0:T(8,128)(2,1)S(1)}, bf16[1344,512]{1,0:T(8,128)(2,1)S(1)}, u32[]{:S(2)}, u32[]{:S(2)}) collective-permute-start(bf16[1344,512]{1,0:T(8,128)(2,1)S(1)} %center.1.refs_0_.refs_2_.refs_4_.refs_5_), channel_id=1, source_target_pairs={{0,1},{1,0},{2,3},{3,2},{4,5},{5,4},{6,7},{7,6},{8,9},{9,8},{10,11... | collective-permute-start | bytes 4128776 | tf_op jit(solution)/shard_map/ppermute | solution.py:313
  45.2 32.9 %collective-permute-start.9 = (bf16[1344,512]{1,0:T(8,128)(2,1)S(1)}, bf16[1344,512]{1,0:T(8,128)(2,1)S(1)}, u32[]{:S(2)}, u32[]{:S(2)}) collective-permute-start(bf16[1344,512]{1,0:T(8,128)(2,1)S(1)} %center.1.refs_0_.refs_2_.refs_4_.refs_5_), channel_id=1, source_target_pairs={{0,2},{1,3},{2,0},{3,1},{4,6},{5,7},{6,4},{7,5},{8,10},{9,11},{10,... | collective-permute-start | bytes 4128776 | tf_op jit(solution)/shard_map/ppermute | solution.py:313
  47.8 8.0 %copy-start = (bf16[1344,512]{1,0:T(8,128)(2,1)}, bf16[1344,512]{1,0:T(8,128)(2,1)S(1)}, u32[]{:S(2)}) copy-start(bf16[1344,512]{1,0:T(8,128)(2,1)S(1)} %collective-permute-done.7.refs_1_) | copy-start | bytes 4128772
  55.8 22.3 %copy-start.6 = (bf16[1344,512]{1,0:T(8,128)(2,1)}, bf16[1344,512]{1,0:T(8,128)(2,1)S(1)}, u32[]{:S(2)}) copy-start(bf16[1344,512]{1,0:T(8,128)(2,1)S(1)} %collective-permute-done.10) | copy-start | bytes 4128772
  77.0 1.1 copy-start.2
  78.1 9.4 %collective-permute-start.12 = (bf16[1344,512]{1,0:T(8,128)(2,1)}, bf16[1344,512]{1,0:T(8,128)(2,1)}, u32[]{:S(2)}, u32[]{:S(2)}) collective-permute-start(bf16[1344,512]{1,0:T(8,128)(2,1)} %collective-permute-done.11.refs_2_), channel_id=1, source_target_pairs={{0,8},{8,0},{16,24},{24,16},{1,9},{9,1},{17,25},{25,17},{2,10},{10... | collective-permute-start | bytes 4128776 | tf_op jit(solution)/shard_map/ppermute | solution.py:313
  78.1 9.4 %copy-start.1 = (bf16[1344,512]{1,0:T(8,128)(2,1)S(1)}, bf16[1344,512]{1,0:T(8,128)(2,1)}, u32[]{:S(2)}) copy-start(bf16[1344,512]{1,0:T(8,128)(2,1)} %copy-done) | copy-start | bytes 4128772
  78.1 9.4 %copy-start.3 = (bf16[1344,512]{1,0:T(8,128)(2,1)S(1)}, bf16[1344,512]{1,0:T(8,128)(2,1)}, u32[]{:S(2)}) copy-start(bf16[1344,512]{1,0:T(8,128)(2,1)} %copy-done.2) | copy-start | bytes 4128772
  78.2 32.3 %collective-permute-start.13 = (bf16[672,512]{1,0:T(8,128)(2,1)S(1)}, bf16[672,512]{1,0:T(8,128)(2,1)S(1)}, u32[]{:S(2)}, u32[]{:S(2)}) collective-permute-start(bf16[672,512]{1,0:T(8,128)(2,1)S(1)} %get-tuple-element.56), channel_id=1, source_target_pairs={{0,6},{6,0},{1,7},{7,1},{8,14},{14,8},{9,15},{15,9},{16,22},{22,16... | collective-permute-start | bytes 2064392 | tf_op jit(solution)/shard_map/ppermute | solution.py:346
  83.0 35.2 %copy-start.7 = (bf16[1344,512]{1,0:T(8,128)(2,1)S(1)}, bf16[1344,512]{1,0:T(8,128)(2,1)}, u32[]{:S(2)}) copy-start(bf16[1344,512]{1,0:T(8,128)(2,1)} %copy-done.6) | copy-start | bytes 4128772
  83.0 31.6 %collective-permute-start.16 = (bf16[672,512]{1,0:T(8,128)(2,1)S(1)}, bf16[672,512]{1,0:T(8,128)(2,1)S(1)}, u32[]{:S(2)}, u32[]{:S(2)}) collective-permute-start(bf16[672,512]{1,0:T(8,128)(2,1)S(1)} %get-tuple-element.55), channel_id=1, source_target_pairs={{0,6},{6,0},{1,7},{7,1},{8,14},{14,8},{9,15},{15,9},{16,22},{22,16... | collective-permute-start | bytes 2064392 | tf_op jit(solution)/shard_map/ppermute | solution.py:346
  86.2 32.1 %collective-permute-start.15 = (bf16[1344,512]{1,0:T(8,128)(2,1)S(1)}, bf16[1344,512]{1,0:T(8,128)(2,1)S(1)}, u32[]{:S(2)}, u32[]{:S(2)}) collective-permute-start(bf16[1344,512]{1,0:T(8,128)(2,1)S(1)} %collective-permute-done.9.refs_6_.refs_1_), channel_id=1, source_target_pairs={{0,1},{1,0},{2,3},{3,2},{4,5},{5,4},{6,7},{7,6},{8,9},{9,8},{10,11... | collective-permute-start | bytes 4128776 | tf_op jit(solution)/shard_map/ppermute | solution.py:313
  118.4 29.5 %collective-permute-start.17 = (bf16[672,512]{1,0:T(8,128)(2,1)S(1)}, bf16[672,512]{1,0:T(8,128)(2,1)S(1)}, u32[]{:S(2)}, u32[]{:S(2)}) collective-permute-start(bf16[672,512]{1,0:T(8,128)(2,1)S(1)} %get-tuple-element.54.refs_3_.refs_1_), channel_id=1, source_target_pairs={{0,1},{1,0},{2,3},{3,2},{4,5},{5,4},{6,7},{7,6},{8,9},{9,8},{10,11... | collective-permute-start | bytes 2064392 | tf_op jit(solution)/shard_map/ppermute | solution.py:313
  119.8 31.8 %collective-permute-start.14 = (bf16[672,512]{1,0:T(8,128)(2,1)S(1)}, bf16[672,512]{1,0:T(8,128)(2,1)S(1)}, u32[]{:S(2)}, u32[]{:S(2)}) collective-permute-start(bf16[672,512]{1,0:T(8,128)(2,1)S(1)} %get-tuple-element.54.refs_3_.refs_1_), channel_id=1, source_target_pairs={{0,2},{1,3},{2,0},{3,1},{4,6},{5,7},{6,4},{7,5},{8,10},{9,11},{10,... | collective-permute-start | bytes 2064392 | tf_op jit(solution)/shard_map/ppermute | solution.py:313
  119.8 30.9 %collective-permute-start.18 = (bf16[672,512]{1,0:T(8,128)(2,1)S(1)}, bf16[672,512]{1,0:T(8,128)(2,1)S(1)}, u32[]{:S(2)}, u32[]{:S(2)}) collective-permute-start(bf16[672,512]{1,0:T(8,128)(2,1)S(1)} %get-tuple-element.53.refs_4_.refs_2_), channel_id=1, source_target_pairs={{0,2},{1,3},{2,0},{3,1},{4,6},{5,7},{6,4},{7,5},{8,10},{9,11},{10,... | collective-permute-start | bytes 2064392 | tf_op jit(solution)/shard_map/ppermute | solution.py:313
  121.8 29.8 %collective-permute-start.21 = (bf16[672,512]{1,0:T(8,128)(2,1)S(1)}, bf16[672,512]{1,0:T(8,128)(2,1)S(1)}, u32[]{:S(2)}, u32[]{:S(2)}) collective-permute-start(bf16[672,512]{1,0:T(8,128)(2,1)S(1)} %get-tuple-element.53.refs_4_.refs_2_), channel_id=1, source_target_pairs={{0,1},{1,0},{2,3},{3,2},{4,5},{5,4},{6,7},{7,6},{8,9},{9,8},{10,11... | collective-permute-start | bytes 2064392 | tf_op jit(solution)/shard_map/ppermute | solution.py:313
  150.6 21.9 %collective-permute-start.19 = (bf16[672,512]{1,0:T(8,128)(2,1)S(1)}, bf16[672,512]{1,0:T(8,128)(2,1)S(1)}, u32[]{:S(2)}, u32[]{:S(2)}) collective-permute-start(bf16[672,512]{1,0:T(8,128)(2,1)S(1)} %collective-permute-done.17.refs_3_), channel_id=1, source_target_pairs={{0,2},{1,3},{2,0},{3,1},{4,6},{5,7},{6,4},{7,5},{8,10},{9,11},{10,... | collective-permute-start | bytes 2064392 | tf_op jit(solution)/shard_map/ppermute | solution.py:313
  150.9 21.6 %collective-permute-start.20 = (bf16[672,512]{1,0:T(8,128)(2,1)S(1)}, bf16[672,512]{1,0:T(8,128)(2,1)S(1)}, u32[]{:S(2)}, u32[]{:S(2)}) collective-permute-start(bf16[672,512]{1,0:T(8,128)(2,1)S(1)} %collective-permute-done.18.refs_6_.refs_2_), channel_id=1, source_target_pairs={{0,1},{1,0},{2,3},{3,2},{4,5},{5,4},{6,7},{7,6},{8,9},{9,8},{10,11... | collective-permute-start | bytes 2064392 | tf_op jit(solution)/shard_map/ppermute | solution.py:313
